TPU v7x, 128 devices: a whole 4x4x4 slice. The times are simulated.
128 devices in a mesh: gx: 8 (over y, core), gy: 16 (over x, z).
Axes of the slice: x: 4, y: 4, z: 4, core: 2. Of those that a mesh axis runs over, the one named last changes fastest.
Arguments:
- field: bfloat16 [20, 128, 128, 1024], P(None, 'gx', 'gy'), may hold values from -6 to 6
- spectral_weight: bfloat16 [2, 128, 20, 20, 1024], P(None, ('gx', 'gy')), may hold values from -1 to 1
- bypass_weight: bfloat16 [20, 20], replicated, may hold values from -1.25 to 1.25
- bypass_bias: float32 [20], replicated, may hold values from -3 to 3
- cotangent: bfloat16 [20, 128, 128, 1024], P(None, 'gx', 'gy'), may hold values from -1.5 to 1.5
Outputs:
- out_field: bfloat16 [20, 128, 128, 1024], P(None, 'gx', 'gy')
- field_grad: bfloat16 [20, 128, 128, 1024], P(None, 'gx', 'gy')
- spectral_grad: bfloat16 [2, 128, 20, 20, 1024], P(None, ('gx', 'gy'))
- bypass_grad: float32 [20, 20], replicated
- bias_grad: float32 [20], replicated
All inputs are finite; a program needn't handle non-finite values.
Results may differ from a plain program's by a relative error of at most 0.022.
Values may be sent and summed in bfloat16 or wider, within the bound.
No kernel may reach another device: no remote copies, remote signals or barrier semaphores. Data moves between devices by JAX's collectives and lax.ppermute only.
A program may use at most 192 MiB of HBM per device.

v0:
```python
import math

import jax
import jax.numpy as jnp
import ml_dtypes
import numpy as np
from jax import lax
from jax.experimental import pallas as pl
from jax.experimental.pallas import tpu as pltpu
from jax.sharding import PartitionSpec as P

NX = 128
NY = 128
NZ = 64
NT = 16
MX = 32
MY = 32
MZ = 16
MT = 8
CH = 20
GX = 8
GY = 16
LX = NX // GX
LY = NY // GY
XY = LX * LY
ZT = NZ * NT
PAIRS = 2 * MZ * MT
MODES = MZ * MT
HI = CH // 4
AXES = ("gx", "gy")
BF = jnp.bfloat16
F32 = jnp.float32
MIB = 1 << 20


def mode_numbers(count):
    index = np.arange(count)
    return np.where(index < count // 2, index, index - count)


def plane_tables():
    z_freq = mode_numbers(MZ)
    t_freq = np.arange(MT)
    turn_z = (np.arange(NZ)[:, None] * z_freq[None, :] % NZ).astype(np.float32) / np.float32(NZ)
    turn_t = (np.arange(NT)[:, None] * t_freq[None, :] % NT).astype(np.float32) / np.float32(NT)
    angle = np.float32(2.0 * math.pi) * (turn_z[:, None, :, None] + turn_t[None, :, None, :])
    parts = np.stack([np.cos(angle), -np.sin(angle)], -1)
    factor = np.where(t_freq == 0, 1.0, 2.0).astype(np.float32)
    forward = parts.reshape(ZT, PAIRS) / np.float32(math.sqrt(ZT))
    inverse = (parts * factor[:, None]).reshape(ZT, PAIRS).T / np.float32(math.sqrt(PAIRS))
    return (forward.astype(ml_dtypes.bfloat16), inverse.astype(ml_dtypes.bfloat16))


def line_parts(length, kept):
    freqs = mode_numbers(kept)
    turns = (freqs[:, None] * np.arange(length)[None, :] % length).astype(np.float32)
    angle = np.float32(2.0 * math.pi / length) * turns
    norm = np.float32(math.sqrt(length))
    return (np.cos(angle) / norm, np.sin(angle) / norm)


def x_table():
    parts = np.stack(line_parts(NX, MX)).reshape(2, MX // 4, 4, GX, LX)
    table = np.einsum("phajw,vz->pvahjwz", parts, np.eye(LY, dtype=np.float32))
    return table.reshape(2 * LY * MX, GX * XY)


def y_table():
    cosine, sine = line_parts(NY, MY)
    block = np.stack(
        [
            np.stack([np.stack([cosine, -sine]), np.stack([sine, cosine])]),
            np.stack([np.stack([-sine, -cosine]), np.stack([cosine, -sine])]),
        ]
    )
    block = block.reshape(2, 2, 2, MY, GY, LY)
    table = np.einsum("sqpbkv,cd->svkcqdpb", block, np.eye(4, dtype=np.float32))
    return table.reshape(2 * LY * GY * 8, 8 * MY)


def spread_table():
    table = np.zeros((4, 4, MY, 4, 4, MY), np.float32)
    for low in range(4):
        for c in range(4):
            table[low, c, :, c, low, :] = np.eye(MY)
    return table.reshape(16 * MY, 16 * MY)


def pack_table(rows):
    table = np.zeros((8, rows, CH, 8, 2), np.float32)
    for m in range(8):
        for ch in range(CH):
            for r in range(2):
                table[m, 2 * ch + r, ch, m, r] = 1
    return table.reshape(8 * rows, CH * 16)


def fold_table():
    table = np.zeros((6, 8, 48), np.float32)
    for slot in range(42):
        table[slot % 6, slot // 6, slot if slot < 21 else slot + 3] = 1
    return table


def const(table):
    return jnp.asarray(np.asarray(table, np.float32).astype(ml_dtypes.bfloat16))


def dot(left, right, dims=((1,), (0,))):
    return lax.dot_general(left, right, (dims, ((), ())), preferred_element_type=F32)


def call(kernel, out, grid=None, limit=32, **kw):
    return pl.pallas_call(
        kernel,
        out_shape=out,
        grid=grid or (),
        compiler_params=pltpu.CompilerParams(vmem_limit_bytes=limit * MIB),
        **kw,
    )


def whole(shape):
    return pl.BlockSpec(shape, lambda *_: (0,) * len(shape))


def pack(coef, perm, out_ref):
    for b in range(0, MODES // 8, 2):
        sides = [coef[:, 16 * (b + e) : 16 * (b + e) + 16].reshape(16 * CH, XY) for e in range(2)]
        moved = dot(perm, jnp.concatenate(sides, 1)).astype(BF)
        for e in range(2):
            out_ref[(b + e) * 320 : (b + e + 1) * 320] = moved[:, e * XY : (e + 1) * XY]


def unpack(msg_ref, perm, rows, flat, coef):
    for b in range(0, MODES // 8, 2):
        sides = [msg_ref[(b + e) * 8 * rows : (b + e + 1) * 8 * rows] for e in range(2)]
        moved = dot(perm, jnp.concatenate(sides, 1)).astype(BF)
        for e in range(2):
            part = moved[:, e * XY : (e + 1) * XY].reshape(CH, 16, XY)
            flat[:, 16 * (b + e) : 16 * (b + e) + 16] = part
    for ch in range(CH):
        coef[ch] = flat[ch].T.reshape(LX, LY, PAIRS)


def first_kernel(field_ref, table_ref, perm_ref, out_ref, flat):
    g = pl.program_id(0)
    block = field_ref.shape[0]
    coef = dot(field_ref[...].reshape(block * XY, ZT), table_ref[...]).astype(BF)
    for c in range(block):
        flat[pl.ds(g * block + c, 1)] = coef[c * XY : (c + 1) * XY].T[None]

    @pl.when(g == pl.num_programs(0) - 1)
    def _():
        pack(flat, perm_ref[...], out_ref)


def plane_stage(field, table, perm):
    block = 4
    return call(
        first_kernel,
        jax.ShapeDtypeStruct((MODES * 2 * CH, XY), BF),
        grid=(CH // block,),
        limit=56,
        in_specs=[
            pl.BlockSpec((block, XY, ZT), lambda g: (g, 0, 0)),
            whole(table.shape),
            whole(perm.shape),
        ],
        out_specs=whole((MODES * 2 * CH, XY)),
        scratch_shapes=[pltpu.VMEM((CH, PAIRS, XY), BF)],
    )(field, table, perm)


def modes_in(msg_ref, x_ref, y_ref, spread_ref, scale):
    rows = [
        jnp.concatenate([msg_ref[j, :, hi].reshape(GY * 8, XY) for j in range(GX)], 1)
        for hi in range(HI)
    ]
    after_x = dot(x_ref[...], jnp.concatenate(rows, 0), ((1,), (1,))).astype(BF)
    left = jnp.concatenate(
        [
            jnp.concatenate(
                [after_x[s * MX : (s + 1) * MX, hi * 128 : (hi + 1) * 128] for s in range(2 * LY)], 1
            )
            for hi in range(HI)
        ],
        0,
    )
    after_y = dot(left, y_ref[...]) * scale
    grouped = jnp.concatenate(
        [
            jnp.concatenate(
                [
                    after_y[hi * MX + 8 * low : hi * MX + 8 * low + 8, t * 128 : (t + 1) * 128]
                    for low in range(4)
                ],
                1,
            )
            for t in range(2)
            for hi in range(HI)
        ],
        0,
    ).astype(BF)
    spread = dot(grouped, spread_ref[...])
    found = {}
    for t in range(2):
        for hi in range(HI):
            for c in range(4):
                at = 4 * t + c
                row = (t * HI + hi) * 8
                found[hi * 4 + at // 2, at % 2] = spread[row : row + 8, c * 128 : (c + 1) * 128]
    return found


def modes_out(found, x_ref, y_back_ref, gather_ref, out_ref):
    rows = []
    for t in range(2):
        for hi in range(HI):
            tiles = []
            for c in range(4):
                at = 4 * t + c
                tiles.append(found[hi * 4 + at // 2, at % 2])
            rows.append(jnp.concatenate(tiles, 1))
    gathered = dot(jnp.concatenate(rows, 0).astype(BF), gather_ref[...])
    grouped = jnp.concatenate(
        [
            jnp.concatenate(
                [
                    gathered[(t * HI + hi) * 8 : (t * HI + hi) * 8 + 8, low * 128 : (low + 1) * 128]
                    for t in range(2)
                ],
                1,
            )
            for hi in range(HI)
            for low in range(4)
        ],
        0,
    ).astype(BF)
    after_y = dot(grouped, y_back_ref[...]).astype(BF)
    left = jnp.concatenate(
        [
            jnp.concatenate(
                [
                    after_y[hi * MX : (hi + 1) * MX, s * 128 : (s + 1) * 128]
                    for hi in range(HI)
                ],
                1,
            )
            for s in range(2 * LY)
        ],
        0,
    )
    after_x = dot(left.T, x_ref[...]).astype(BF)
    for j in range(GX):
        for hi in range(HI):
            block = after_x[hi * 128 : (hi + 1) * 128, j * XY : (j + 1) * XY]
            out_ref[j, :, hi] = block.reshape(GY, 8, XY)


def mix_kernel(msg_ref, w_ref, x_ref, y_ref, y_back_ref, spread_ref, gather_ref, out_ref, spec_ref):
    spec = modes_in(msg_ref, x_ref, y_ref, spread_ref, 1.0)
    for i in range(CH):
        for r in range(2):
            spec_ref[i, r] = spec[i, r]
    mixed = {}
    for o in range(CH):
        real = jnp.zeros((8, 128), F32)
        imag = jnp.zeros((8, 128), F32)
        for i in range(CH):
            w_real = w_ref[0, i, o].astype(F32)
            w_imag = w_ref[1, i, o].astype(F32)
            real += w_real * spec[i, 0] - w_imag * spec[i, 1]
            imag += w_real * spec[i, 1] + w_imag * spec[i, 0]
        mixed[o, 0] = 4.0 * real
        mixed[o, 1] = 4.0 * imag
    modes_out(mixed, x_ref, y_back_ref, gather_ref, out_ref)


def mix_back_kernel(
    msg_ref, w_ref, spec_ref, sums_ref, x_ref, y_ref, y_back_ref, spread_ref, gather_ref, out_ref, grad_ref
):
    back = modes_in(msg_ref, x_ref, y_ref, spread_ref, 4.0)
    mixed = {}
    for i in range(CH):
        real = jnp.zeros((8, 128), F32)
        imag = jnp.zeros((8, 128), F32)
        in_real = spec_ref[i, 0]
        in_imag = spec_ref[i, 1]
        for o in range(CH):
            w_real = w_ref[0, i, o].astype(F32)
            w_imag = w_ref[1, i, o].astype(F32)
            real += w_real * back[o, 0] + w_imag * back[o, 1]
            imag += w_real * back[o, 1] - w_imag * back[o, 0]
            grad_ref[0, i, o] = (in_real * back[o, 0] + in_imag * back[o, 1]).astype(BF)
            grad_ref[1, i, o] = (in_real * back[o, 1] - in_imag * back[o, 0]).astype(BF)
        mixed[i, 0] = real
        mixed[i, 1] = imag
    modes_out(mixed, x_ref, y_back_ref, gather_ref, out_ref)
    for j in range(GX):
        out_ref[j, :, HI] = jnp.broadcast_to(sums_ref[...][None], (GY, 8, XY))


def tail_kernel(
    msg_ref, field_ref, cot_ref, mix_ref, bias_ref, perm_ref, pack_ref, inv_ref, back_ref, fold_ref,
    out_ref, grad_ref, coef_ref, sums_ref, flat, coef, back_coef, weight_sum,
):
    g = pl.program_id(0)
    block = field_ref.shape[1]

    @pl.when(g == 0)
    def _():
        unpack(msg_ref, perm_ref[...], 2 * CH, flat, coef)
        weight_sum[...] = jnp.zeros_like(weight_sum)

    total = jnp.zeros(weight_sum.shape, F32)
    for e in range(block):
        field = field_ref[:, e].reshape(CH * LY, ZT)
        left = coef[:, pl.ds(g * block + e, 1)].reshape(CH * LY, PAIRS)
        pre = dot(left, inv_ref[...]) + dot(mix_ref[...], field) + bias_ref[...]
        cot = cot_ref[:, e].reshape(CH * LY, ZT).astype(F32)
        square = pre * pre
        root = math.sqrt(2.0 / math.pi)
        bend = jnp.tanh(pre * (root + (root * 0.044715) * square))
        half = 0.5 + 0.5 * bend
        out_ref[:, e] = (pre * half).astype(BF).reshape(CH, LY, ZT)
        slope = half + (0.5 * pre) * ((1.0 - bend * bend) * (root + (3.0 * root * 0.044715) * square))
        grad = (cot * slope).astype(BF)
        grad_ref[:, e] = grad.reshape(CH, LY, ZT)
        back = dot(grad, back_ref[...]).astype(BF)
        back_coef[:, pl.ds(g * block + e, 1)] = back.reshape(CH, 1, LY, PAIRS)
        ones = jnp.concatenate([field, jnp.ones((16, ZT), BF)], 0)
        total += dot(ones, grad, ((1,), (1,)))
    weight_sum[...] += total

    @pl.when(g == pl.num_programs(0) - 1)
    def _():
        for ch in range(CH):
            flat[ch] = back_coef[ch].reshape(XY, PAIRS).T
        pack(flat, pack_ref[...], coef_ref)
        summed = weight_sum[...]
        rows = lax.broadcasted_iota(jnp.int32, summed.shape, 0)
        lanes = lax.broadcasted_iota(jnp.int32, summed.shape, 1)
        keep = (rows >= CH * LY) | (rows % LY == lanes % LY)
        by_row = jnp.where(keep, summed, 0.0)
        by_row = by_row.reshape(CH + 2, LY, CH * LY)
        by_row = jnp.concatenate(
            [jnp.sum(by_row[:CH], 1), by_row[CH, :1], jnp.zeros((3, CH * LY), F32)], 0
        )
        at = lax.broadcasted_iota(jnp.int32, (CH * LY, 128), 0) // LY
        to = lax.broadcasted_iota(jnp.int32, (CH * LY, 128), 1)
        gather = jnp.where(at == to, 1.0, 0.0)
        full = lax.dot_general(
            by_row, gather, (((1,), (0,)), ((), ())),
            precision=lax.Precision.HIGHEST, preferred_element_type=F32,
        )
        high = full.astype(BF)
        low = (full - high.astype(F32)).astype(BF)
        both = jnp.concatenate([high.astype(F32), low.astype(F32)], 0).astype(BF)
        folded = jnp.zeros((8, 128), F32)
        for s in range(6):
            folded += pltpu.roll(dot(fold_ref[s], both), CH * s, 1)
        sums_ref[...] = folded.astype(BF)


def last_kernel(
    msg_ref, grad_ref, mix_ref, perm_ref, table_ref, fold_ref, out_ref, sums_ref, flat, coef
):
    g = pl.program_id(0)
    block = grad_ref.shape[1]

    @pl.when(g == 0)
    def _():
        unpack(msg_ref, perm_ref[...], 48, flat, coef)
        summed = jnp.zeros((8, 128), F32)
        for m in range(MODES):
            summed += msg_ref[m * 48 + 40 : m * 48 + 48].astype(F32)
        lanes = lax.broadcasted_iota(jnp.int32, (8, 128), 1)
        full = jnp.zeros((48, 128), F32)
        for s in range(6):
            part = jnp.where(lanes < CH, pltpu.roll(summed, (128 - CH * s) % 128, 1), 0.0)
            full += lax.dot_general(
                fold_ref[s].astype(F32), part, (((0,), (0,)), ((), ())),
                precision=lax.Precision.HIGHEST, preferred_element_type=F32,
            )
        sums_ref[...] = (full[:24] + full[24:]) * (1.0 / math.sqrt(NX * NY * ZT))

    for e in range(block):
        left = coef[:, pl.ds(g * block + e, 1)].reshape(CH * LY, PAIRS)
        grad = grad_ref[:, e].reshape(CH * LY, ZT)
        total = dot(left, table_ref[...]) + dot(mix_ref[...], grad)
        out_ref[:, e] = total.astype(BF).reshape(CH, LY, ZT)


def exchange(messages):
    return lax.all_to_all(messages, AXES, split_axis=0, concat_axis=0, tiled=True)


def local(field, spectral_weight, bypass_weight, bypass_bias, cotangent):
    fwd_zt, inv_zt = plane_tables()
    x_parts = const(x_table())
    y_parts = const(y_table())
    y_back = const(y_table().T)
    spread = const(spread_table())
    gather = const(spread_table().T)
    perm = const(pack_table(40))
    perm_back = const(pack_table(40).T)
    perm_wide = const(pack_table(48).T)
    folds = const(fold_table())
    eye = jnp.eye(LY, dtype=BF)
    mix_in = jnp.kron(bypass_weight, eye)
    mix_out = jnp.kron(bypass_weight.T, eye)
    bias = jnp.repeat(bypass_bias, LY)[:, None]
    weight = spectral_weight.reshape(2, CH, CH, 8, 128)
    tiles = (GX, GY, HI, 8, XY)

    plane = plane_stage(field.reshape(CH, XY, ZT), const(fwd_zt), perm)
    arrived = exchange(plane.reshape(MODES, 2 * CH, XY))
    sent, spec = call(
        mix_kernel,
        (jax.ShapeDtypeStruct(tiles, BF), jax.ShapeDtypeStruct((CH, 2, 8, 128), F32)),
    )(arrived.reshape(tiles), weight, x_parts, y_parts, y_back, spread, gather)
    arrived = exchange(sent.reshape(MODES, 2 * CH, XY))

    block = 2
    cells = pl.BlockSpec((CH, block, LY, ZT), lambda g: (0, g, 0, 0))
    grid_shape = jax.ShapeDtypeStruct((CH, LX, LY, ZT), BF)
    out_field, grad_pre, back_coef, sums = call(
        tail_kernel,
        (
            grid_shape,
            grid_shape,
            jax.ShapeDtypeStruct((MODES * 2 * CH, XY), BF),
            jax.ShapeDtypeStruct((8, 128), BF),
        ),
        grid=(LX // block,),
        limit=56,
        in_specs=[
            whole((MODES * 2 * CH, XY)),
            cells,
            cells,
            whole((CH * LY, CH * LY)),
            whole((CH * LY, 1)),
            whole(perm.shape),
            whole(perm.shape),
            whole((PAIRS, ZT)),
            whole((ZT, PAIRS)),
            whole(folds.shape),
        ],
        out_specs=[cells, cells, whole((MODES * 2 * CH, XY)), whole((8, 128))],
        scratch_shapes=[
            pltpu.VMEM((CH, PAIRS, XY), BF),
            pltpu.VMEM((CH, LX, LY, PAIRS), BF),
            pltpu.VMEM((CH, LX, LY, PAIRS), BF),
            pltpu.VMEM((CH * LY + 16, CH * LY), F32),
        ],
    )(
        arrived.reshape(MODES * 2 * CH, XY), field, cotangent, mix_out, bias, perm_back, perm,
        const(inv_zt), const(inv_zt.T), folds,
    )

    arrived = exchange(back_coef.reshape(MODES, 2 * CH, XY))
    sent, spectral_grad = call(
        mix_back_kernel,
        (
            jax.ShapeDtypeStruct((GX, GY, HI + 1, 8, XY), BF),
            jax.ShapeDtypeStruct((2, CH, CH, 8, 128), BF),
        ),
    )(arrived.reshape(tiles), weight, spec, sums, x_parts, y_parts, y_back, spread, gather)
    arrived = exchange(sent.reshape(MODES, 48, XY))

    block = 4
    cells = pl.BlockSpec((CH, block, LY, ZT), lambda g: (0, g, 0, 0))
    field_grad, totals = call(
        last_kernel,
        (grid_shape, jax.ShapeDtypeStruct((24, 128), F32)),
        grid=(LX // block,),
        limit=56,
        in_specs=[
            whole((MODES * 48, XY)),
            cells,
            whole((CH * LY, CH * LY)),
            whole(perm_wide.shape),
            whole((PAIRS, ZT)),
            whole(folds.shape),
        ],
        out_specs=[cells, whole((24, 128))],
        scratch_shapes=[pltpu.VMEM((CH, PAIRS, XY), BF), pltpu.VMEM((CH, LX, LY, PAIRS), BF)],
    )(arrived.reshape(MODES * 48, XY), grad_pre, mix_in, perm_wide, const(fwd_zt.T), folds)
    spectral_grad = spectral_grad.reshape(spectral_weight.shape)
    return (out_field, field_grad, spectral_grad, totals[:CH, :CH], totals[CH, :CH])


def solution(mesh):
    in_specs = (
        P(None, "gx", "gy", None),
        P(None, AXES, None, None, None),
        P(),
        P(),
        P(None, "gx", "gy", None),
    )
    out_specs = (
        P(None, "gx", "gy", None),
        P(None, "gx", "gy", None),
        P(None, AXES, None, None, None),
        P(),
        P(),
    )
    return jax.shard_map(local, mesh=mesh, in_specs=in_specs, out_specs=out_specs, check_vma=False)
```

profile of v0, /device:TPU:0, one launch (start us, length us, event | category | flops | bytes accessed | tf_op | source)
XLA Modules:
  0.0 170.7 jit_solution(3701490762243048182)
XLA Ops:
  0.6 7.3 %shard_map.209 = bf16[5120,128]{1,0:T(8,128)(2,1)} custom-call(bf16[20,128,1024]{2,1,0:T(8,128)(2,1)} %bitcast.21, bf16[1024,256]{1,0:T(8,128)(2,1)} %constant.32.clone.table_ref, bf16[320,320]{1,0:T(8,128)(2,1)} %constant.28.clone.perm_ref.pack_ref), custom_call_target="tpu_custom_call" | custom-call | tf_op jit(solution)/shard_map/pallas_call | solution.py:160
  7.9 11.1 %all-to-all-start = ((bf16[128,40,128]{2,1,0:T(8,128)(2,1)}), bf16[128,40,128]{2,1,0:T(8,128)(2,1)S(1)}, u32[]{:S(2)}, u32[]{:S(2)}) async-start(bf16[128,40,128]{2,1,0:T(8,128)(2,1)} %bitcast.23), calls=%async_computation | async-start | bytes 2621440 | tf_op jit(solution)/shard_map/all_to_all | solution.py:396
  19.1 2.0 %reshape.65 = bf16[2,20,20,8,128]{4,3,0,2,1:T(8,128)(2,1)} reshape(bf16[2,1,20,20,1024]{4,0,3,2,1:T(2,128)(2,1)S(1)} %copy-done.16) | data formatting | bytes 3276800 | tf_op jit(solution)/shard_map/reshape | solution.py:414
  21.1 1.8 %copy.26.w_ref = bf16[2,20,20,8,128]{4,3,2,1,0:T(8,128)(2,1)S(1)} copy(bf16[2,20,20,8,128]{4,3,0,2,1:T(8,128)(2,1)} %reshape.65) | data formatting | bytes 3276800 | tf_op jit(solution)/shard_map/reshape | solution.py:414
  22.8 18.0 %all-to-all-done = bf16[128,40,128]{2,1,0:T(8,128)(2,1)S(1)} async-done(((bf16[128,40,128]{2,1,0:T(8,128)(2,1)}), bf16[128,40,128]{2,1,0:T(8,128)(2,1)S(1)}, u32[]{:S(2)}, u32[]{:S(2)}) %all-to-all-start) | async-done | bytes 1310752 | tf_op jit(solution)/shard_map/all_to_all | solution.py:396
  40.9 1.2 copy-done.1
  42.1 1.2 copy-done.3
  43.3 1.2 copy-done.5
  44.5 3.6 %shard_map.210 = (bf16[8,16,5,8,128]{4,3,2,1,0:T(8,128)(2,1)S(1)}, f32[20,2,8,128]{3,2,1,0:T(8,128)S(1)}) custom-call(bf16[8,16,5,8,128]{4,3,2,1,0:T(8,128)(2,1)S(1)} %bitcast.17, bf16[2,20,20,8,128]{4,3,2,1,0:T(8,128)(2,1)S(1)} %copy.26.w_ref, bf16[512,1024]{1,0:T(8,128)(2,1)S(1)} %copy-done.5, bf16[2048,256]{1,0:T(8,128)(2,1)S(1)} %copy-done.3, ...), custom_call_target="tpu_custom_call" | custom-call | tf_op jit(solution)/shard_map/pallas_call | solution.py:419
  48.1 1.0 copy-done.10
  49.2 0.7 copy-done.11
  49.8 4.8 %all-to-all-start.1 = ((bf16[128,40,128]{2,1,0:T(8,128)(2,1)}), bf16[128,40,128]{2,1,0:T(8,128)(2,1)S(1)}, u32[]{:S(2)}, u32[]{:S(2)}) async-start(bf16[128,40,128]{2,1,0:T(8,128)(2,1)} %bitcast.20), calls=%async_computation.1 | async-start | bytes 2621440 | tf_op jit(solution)/shard_map/all_to_all | solution.py:396
  54.6 0.1 copy.27
  54.7 0.1 broadcast_in_dim.9
  54.8 0.7 broadcast_in_dim_reshape.4.bias_ref
  55.5 1.5 broadcast_multiply_fusion
  57.0 2.4 %mul.44.mix_ref = bf16[160,160]{1,0:T(8,128)(2,1)} reshape(bf16[20,8,20,8]{3,2,1,0:T(8,128)(2,1)} %get-tuple-element.31) | data formatting | bytes 102400 | tf_op jit(solution)/shard_map/jit(kron)/mul | solution.py:412
  59.5 16.9 %all-to-all-done.1 = bf16[128,40,128]{2,1,0:T(8,128)(2,1)S(1)} async-done(((bf16[128,40,128]{2,1,0:T(8,128)(2,1)}), bf16[128,40,128]{2,1,0:T(8,128)(2,1)S(1)}, u32[]{:S(2)}, u32[]{:S(2)}) %all-to-all-start.1) | async-done | bytes 1310752 | tf_op jit(solution)/shard_map/all_to_all | solution.py:396
  76.4 1.1 copy-done.15
  77.4 19.6 %shard_map.211 = (bf16[20,16,8,1024]{3,2,1,0:T(8,128)(2,1)}, bf16[20,16,8,1024]{3,2,1,0:T(8,128)(2,1)}, bf16[5120,128]{1,0:T(8,128)(2,1)}, bf16[8,128]{1,0:T(8,128)(2,1)}) custom-call(bf16[5120,128]{1,0:T(8,128)(2,1)} %bitcast.24, bf16[20,16,8,1024]{3,2,1,0:T(8,128)(2,1)} %field_ref.1, bf16[20,16,8,1024]{3,2,1,0:T(8,128)(2,1)} %cot_ref.1, ...), custom_call_target="tpu_custom_call" | custom-call | tf_op jit(solution)/shard_map/pallas_call | solution.py:428
  97.1 26.8 %all_to_all.20 = bf16[128,40,128]{2,1,0:T(8,128)(2,1)S(1)} all-to-all(bf16[128,40,128]{2,1,0:T(8,128)(2,1)} %bitcast.25), channel_id=1, replica_groups=mesh['gx'=8,'gy'=16] {'gx','gy'}, dimensions={0} | all-to-all | bytes 2621440 | tf_op jit(solution)/shard_map/all_to_all | solution.py:396
  123.9 4.1 %shard_map.212 = (bf16[8,16,6,8,128]{4,3,2,1,0:T(8,128)(2,1)S(1)}, bf16[2,20,20,8,128]{4,3,2,1,0:T(8,128)(2,1)S(1)}) custom-call(bf16[8,16,5,8,128]{4,3,2,1,0:T(8,128)(2,1)S(1)} %bitcast.18, bf16[2,20,20,8,128]{4,3,2,1,0:T(8,128)(2,1)S(1)} %copy.26.w_ref, f32[20,2,8,128]{3,2,1,0:T(8,128)S(1)} %copy-done.12, bf16[8,128]{1,0:T(8,128)(2,1)S(1)} %copy-done.13, ...), custom_call_target="tpu_custom_call" | custom-call | tf_op jit(solution)/shard_map/pallas_call | solution.py:463
  128.0 1.2 copy-done.7
  129.2 1.2 copy-done.9
  130.4 4.8 %all-to-all-start.3 = ((bf16[128,48,128]{2,1,0:T(8,128)(2,1)}), bf16[128,48,128]{2,1,0:T(8,128)(2,1)S(1)}, u32[]{:S(2)}, u32[]{:S(2)}) async-start(bf16[128,48,128]{2,1,0:T(8,128)(2,1)} %bitcast.19), calls=%async_computation.3 | async-start | bytes 3145728 | tf_op jit(solution)/shard_map/all_to_all | solution.py:396
  135.1 2.4 %mul.47.mix_ref = bf16[160,160]{1,0:T(8,128)(2,1)} reshape(bf16[20,8,20,8]{3,2,1,0:T(8,128)(2,1)} %get-tuple-element.30) | data formatting | bytes 102400 | tf_op jit(solution)/shard_map/jit(kron)/mul | solution.py:411
  137.6 1.9 %reshape.73 = bf16[2,1,20,20,1024]{4,3,2,0,1:T(8,128)(2,1)} reshape(bf16[2,20,20,8,128]{4,3,2,1,0:T(8,128)(2,1)S(1)} %copy-done.8) | data formatting | bytes 3276800 | tf_op jit(solution)/shard_map/reshape | solution.py:490
  139.5 4.4 %copy.31 = bf16[2,1,20,20,1024]{4,0,3,2,1:T(2,128)(2,1)} copy(bf16[2,1,20,20,1024]{4,3,2,0,1:T(8,128)(2,1)} %reshape.73) | data formatting | bytes 3276800 | tf_op jit(solution)/shard_map/reshape | solution.py:490
  143.9 15.7 %all-to-all-done.3 = bf16[128,48,128]{2,1,0:T(8,128)(2,1)S(1)} async-done(((bf16[128,48,128]{2,1,0:T(8,128)(2,1)}), bf16[128,48,128]{2,1,0:T(8,128)(2,1)S(1)}, u32[]{:S(2)}, u32[]{:S(2)}) %all-to-all-start.3) | async-done | bytes 1572896 | tf_op jit(solution)/shard_map/all_to_all | solution.py:396
  159.6 1.2 copy-done.14
  160.8 8.7 %shard_map.213 = (bf16[20,16,8,1024]{3,2,1,0:T(8,128)(2,1)}, f32[24,128]{1,0:T(8,128)}) custom-call(bf16[6144,128]{1,0:T(8,128)(2,1)} %bitcast.22, bf16[20,16,8,1024]{3,2,1,0:T(8,128)(2,1)} %get-tuple-element.21.grad_ref, bf16[160,160]{1,0:T(8,128)(2,1)} %mul.47.mix_ref, bf16[320,384]{1,0:T(8,128)(2,1)} %constant.30.clone.perm_ref, ...), custom_call_target="tpu_custom_call" | custom-call | tf_op jit(solution)/shard_map/pallas_call | solution.py:474
  169.5 1.2 slice_bitcast_fusion
  (30 shorter events, 0.1 us)
Async XLA Ops:
  7.9 11.2 %copy-start.16 = (bf16[2,1,20,20,1024]{4,0,3,2,1:T(2,128)(2,1)S(1)}, bf16[2,1,20,20,1024]{4,0,3,2,1:T(2,128)(2,1)}, u32[]{:S(2)}) copy-start(bf16[2,1,20,20,1024]{4,0,3,2,1:T(2,128)(2,1)} %param.19) | copy-start | bytes 4915204
  7.9 32.9 %all-to-all-start = ((bf16[128,40,128]{2,1,0:T(8,128)(2,1)}), bf16[128,40,128]{2,1,0:T(8,128)(2,1)S(1)}, u32[]{:S(2)}, u32[]{:S(2)}) async-start(bf16[128,40,128]{2,1,0:T(8,128)(2,1)} %bitcast.23), calls=%async_computation | async-start | bytes 2621440 | tf_op jit(solution)/shard_map/all_to_all | solution.py:396
  21.1 19.8 %copy-start = (bf16[512,512]{1,0:T(8,128)(2,1)S(1)}, bf16[512,512]{1,0:T(8,128)(2,1)}, u32[]{:S(2)}) copy-start(bf16[512,512]{1,0:T(8,128)(2,1)} %constant.27.clone.spread_ref.gather_ref) | copy-start | bytes 1572868
  40.9 1.2 copy-start.1
  42.1 1.2 copy-start.3
  43.3 1.2 copy-start.5
  48.1 1.1 copy-start.10
  49.2 0.7 copy-start.11
  49.8 4.8 %copy-start.17 = (bf16[20,20]{1,0:T(8,128)(2,1)S(1)}, bf16[20,20]{1,0:T(8,128)(2,1)}, u32[]{:S(2)}) copy-start(bf16[20,20]{1,0:T(8,128)(2,1)} %param.20) | copy-start | bytes 2404
  49.8 4.9 %copy-start.18 = (f32[20]{0:T(128)S(1)}, f32[20]{0:T(128)}, u32[]{:S(2)}) copy-start(f32[20]{0:T(128)} %param.21) | copy-start | bytes 244
  49.8 26.5 %all-to-all-start.1 = ((bf16[128,40,128]{2,1,0:T(8,128)(2,1)}), bf16[128,40,128]{2,1,0:T(8,128)(2,1)S(1)}, u32[]{:S(2)}, u32[]{:S(2)}) async-start(bf16[128,40,128]{2,1,0:T(8,128)(2,1)} %bitcast.20), calls=%async_computation.1 | async-start | bytes 2621440 | tf_op jit(solution)/shard_map/all_to_all | solution.py:396
  76.4 1.1 copy-start.15
  77.4 46.5 %copy-start.6 = (bf16[512,1024]{1,0:T(8,128)(2,1)S(1)}, bf16[512,1024]{1,0:T(8,128)(2,1)}, u32[]{:S(2)}) copy-start(bf16[512,1024]{1,0:T(8,128)(2,1)} %constant.24.clone.x_ref) | copy-start | bytes 3145732
  97.1 26.8 %copy-start.2 = (bf16[256,2048]{1,0:T(8,128)(2,1)S(1)}, bf16[256,2048]{1,0:T(8,128)(2,1)}, u32[]{:S(2)}) copy-start(bf16[256,2048]{1,0:T(8,128)(2,1)} %constant.26.clone.y_back_ref) | copy-start | bytes 3145732
  97.1 26.8 %copy-start.4 = (bf16[2048,256]{1,0:T(8,128)(2,1)S(1)}, bf16[2048,256]{1,0:T(8,128)(2,1)}, u32[]{:S(2)}) copy-start(bf16[2048,256]{1,0:T(8,128)(2,1)} %constant.25.clone.y_ref) | copy-start | bytes 3145732
  97.1 26.8 %copy-start.12 = (f32[20,2,8,128]{3,2,1,0:T(8,128)S(1)}, f32[20,2,8,128]{3,2,1,0:T(8,128)}, u32[]{:S(2)}) copy-start(f32[20,2,8,128]{3,2,1,0:T(8,128)} %copy-done.11) | copy-start | bytes 491524
  97.1 26.8 %copy-start.13 = (bf16[8,128]{1,0:T(8,128)(2,1)S(1)}, bf16[8,128]{1,0:T(8,128)(2,1)}, u32[]{:S(2)}) copy-start(bf16[8,128]{1,0:T(8,128)(2,1)} %get-tuple-element.19.sums_ref) | copy-start | bytes 6148
  128.0 1.2 copy-start.7
  129.2 1.2 copy-start.9
  130.4 7.2 %copy-start.8 = (bf16[2,20,20,8,128]{4,3,2,1,0:T(8,128)(2,1)S(1)}, bf16[2,20,20,8,128]{4,3,2,1,0:T(8,128)(2,1)}, u32[]{:S(2)}) copy-start(bf16[2,20,20,8,128]{4,3,2,1,0:T(8,128)(2,1)} %copy-done.7) | copy-start | bytes 4915204
  130.4 29.2 %all-to-all-start.3 = ((bf16[128,48,128]{2,1,0:T(8,128)(2,1)}), bf16[128,48,128]{2,1,0:T(8,128)(2,1)S(1)}, u32[]{:S(2)}, u32[]{:S(2)}) async-start(bf16[128,48,128]{2,1,0:T(8,128)(2,1)} %bitcast.19), calls=%async_computation.3 | async-start | bytes 3145728 | tf_op jit(solution)/shard_map/all_to_all | solution.py:396
  159.6 1.2 copy-start.14
where the time goes:
time: 172 us; the launch traced here: 171 us
  waiting for transfers between devices  50.7 us (29%)
  Pallas kernels  43.3 us (25%)
  local copies, waits for them, and re-layouts  27 us (16%)
  blocking collectives  26.8 us (16%)
  starting transfers between devices  20.7 us (12%)
    all_to_all x3, waiting for transfers between devices, exchange(): lax.all_to_all(messages, AXES, split_axis=0, concat_axis=0, tiled=True)  50.7 us
    all_to_all x1, blocking collectives, exchange(): lax.all_to_all(messages, AXES, split_axis=0, concat_axis=0, tiled=True)  26.8 us
    all_to_all x3, starting transfers between devices, exchange(): lax.all_to_all(messages, AXES, split_axis=0, concat_axis=0, tiled=True)  20.7 us
    pallas_call x1, Pallas kernels, local(): call(tail_kernel, (grid_shape, grid_shape, jax.ShapeDtypeStruct((MODES *...  19.6 us
    unnamed x38, local copies, waits for them, and re-layouts  10 us
    pallas_call x1, Pallas kernels, local(): call(last_kernel, (grid_shape, jax.ShapeDtypeStruct((24, 128), F32)), gri...  8.73 us
    pallas_call x1, Pallas kernels, plane_stage(): call(first_kernel, jax.ShapeDtypeStruct((MODES * 2 * CH, XY), BF), grid=(...  7.3 us
    reshape x2, local copies, waits for them, and re-layouts, local(): spectral_grad = spectral_grad.reshape(spectral_weight.shape)  6.29 us
  transfers between devices with their start and end apart: 3, of which 3 were waited for; matrix products, arithmetic and copies ran while one was open for 10% of the time, Pallas kernels for 0%

commit v1 on v0

v1 whole, which is shorter than its diff:
```python
import functools
import math

import jax
import jax.numpy as jnp
import ml_dtypes
import numpy as np
from jax import lax
from jax.experimental import pallas as pl
from jax.experimental.pallas import tpu as pltpu
from jax.sharding import PartitionSpec as P

NX = 128
NY = 128
NZ = 64
NT = 16
MX = 32
MY = 32
MZ = 16
MT = 8
CH = 20
GX = 8
GY = 16
LX = NX // GX
LY = NY // GY
XY = LX * LY
ZT = NZ * NT
PAIRS = 2 * MZ * MT
MODES = MZ * MT
HI = CH // 4
AXES = ("gx", "gy")
BF = jnp.bfloat16
F32 = jnp.float32
MIB = 1 << 20
LIMITS = (51, 51, 51, 51)
U = (8, 8, 5, 2)
LANES = 256


def mode_numbers(count):
    index = np.arange(count)
    return np.where(index < count // 2, index, index - count)


def plane_tables():
    z_freq = mode_numbers(MZ)
    t_freq = np.arange(MT)
    turn_z = (np.arange(NZ)[:, None] * z_freq[None, :] % NZ).astype(np.float32) / np.float32(NZ)
    turn_t = (np.arange(NT)[:, None] * t_freq[None, :] % NT).astype(np.float32) / np.float32(NT)
    angle = np.float32(2.0 * math.pi) * (turn_z[:, None, :, None] + turn_t[None, :, None, :])
    parts = np.stack([np.cos(angle), -np.sin(angle)], -1)
    factor = np.where(t_freq == 0, 1.0, 2.0).astype(np.float32)
    forward = parts.reshape(ZT, PAIRS) / np.float32(math.sqrt(ZT))
    inverse = (parts * factor[:, None]).reshape(ZT, PAIRS).T / np.float32(math.sqrt(PAIRS))
    return (forward.astype(ml_dtypes.bfloat16), inverse.astype(ml_dtypes.bfloat16))


def line_parts(length, kept):
    freqs = mode_numbers(kept)
    turns = (freqs[:, None] * np.arange(length)[None, :] % length).astype(np.float32)
    angle = np.float32(2.0 * math.pi / length) * turns
    norm = np.float32(math.sqrt(length))
    return (np.cos(angle) / norm, np.sin(angle) / norm)


def x_table():
    parts = np.stack(line_parts(NX, MX)).reshape(2, MX // 4, 4, GX, LX)
    table = np.einsum("phajw,vz->pvahjwz", parts, np.eye(LY, dtype=np.float32))
    return table.reshape(2 * LY * MX, GX * XY)


def y_table():
    cosine, sine = line_parts(NY, MY)
    block = np.stack(
        [
            np.stack([np.stack([cosine, -sine]), np.stack([sine, cosine])]),
            np.stack([np.stack([-sine, -cosine]), np.stack([cosine, -sine])]),
        ]
    )
    block = block.reshape(2, 2, 2, MY, GY, LY)
    table = np.einsum("sqpbkv,cd->svkcqdpb", block, np.eye(4, dtype=np.float32))
    return table.reshape(2 * LY * GY * 8, 8 * MY)


def spread_table():
    table = np.zeros((4, 4, MY, 4, 4, MY), np.float32)
    for low in range(4):
        for c in range(4):
            table[low, c, :, c, low, :] = np.eye(MY)
    return table.reshape(16 * MY, 16 * MY)


def pack_table(rows):
    table = np.zeros((8, rows, CH, 8, 2), np.float32)
    for m in range(8):
        for ch in range(CH):
            for r in range(2):
                table[m, 2 * ch + r, ch, m, r] = 1
    return table.reshape(8 * rows, CH * 16)


def fold_table():
    table = np.zeros((6, 8, 48), np.float32)
    for slot in range(42):
        table[slot % 6, slot // 6, slot if slot < 21 else slot + 3] = 1
    return table


def const(table):
    return jnp.asarray(np.asarray(table, np.float32).astype(ml_dtypes.bfloat16))


def dot(left, right, dims=((1,), (0,))):
    return lax.dot_general(left, right, (dims, ((), ())), preferred_element_type=F32)


def call(kernel, out, limit=28, cost=None, **kw):
    if cost is not None:
        cost = pl.CostEstimate(flops=cost[0], bytes_accessed=cost[1], transcendentals=0)
    return pl.pallas_call(
        kernel,
        out_shape=out,
        cost_estimate=cost,
        compiler_params=pltpu.CompilerParams(vmem_limit_bytes=int(limit * MIB)),
        **kw,
    )


VMEM = pl.BlockSpec(memory_space=pltpu.VMEM)
HBM = pl.BlockSpec(memory_space=pltpu.HBM)


def pack(coef, perm_ref, stage, out_ref, sems):
    def sent(b):
        rows = pl.ds(pl.multiple_of(b * 640, 640), 640)
        return pltpu.make_async_copy(stage.at[rows], out_ref.at[rows], sems.at[b])

    def step(b, carry):
        both = coef[:, pl.ds(pl.multiple_of(b * 32, 32), 32)]
        sides = [both[:, 16 * e : 16 * e + 16].reshape(16 * CH, XY) for e in range(2)]
        moved = dot(perm_ref[:, :320], jnp.concatenate(sides, 1)).astype(BF)
        for e in range(2):
            at = pl.multiple_of(b * 640 + e * 320, 320)
            stage[pl.ds(at, 320)] = moved[:, e * XY : (e + 1) * XY]
        sent(b).start()
        return carry

    def wait(b, carry):
        sent(b).wait()
        return carry

    lax.fori_loop(0, MODES // 16, step, 0, unroll=U[0])
    lax.fori_loop(0, MODES // 16, wait, 0, unroll=8)


def unpack(msg_ref, perm_ref, rows, flat, coef):
    def step(b, carry):
        sides = []
        for e in range(2):
            at = pl.multiple_of((2 * b + e) * 8 * rows, 8 * rows)
            sides.append(msg_ref[pl.ds(at, 8 * rows)])
        moved = dot(perm_ref[:, : 8 * rows], jnp.concatenate(sides, 1)).astype(BF)
        for e in range(2):
            part = moved[:, e * XY : (e + 1) * XY].reshape(CH, 16, XY)
            flat[:, pl.ds(pl.multiple_of(b * 32 + 16 * e, 16), 16)] = part
        return carry

    def turn(n, carry):
        for e in range(4):
            ch = n * 4 + e
            coef[pl.ds(ch, 1)] = flat[ch].T[None]
        return carry

    lax.fori_loop(0, MODES // 16, step, 0, unroll=U[1])
    lax.fori_loop(0, CH // 4, turn, 0, unroll=U[2])


def load(pairs, sems):
    moved = [pltpu.make_async_copy(s, t, sems.at[n]) for n, (s, t) in enumerate(pairs)]
    for copy in moved:
        copy.start()
    return moved


def first_kernel(
    field_hbm, table_hbm, perm_hbm, out_ref, field, table, perm, flat, stage, in_sems, field_sems, sems
):
    block = 4

    def part_copy(g):
        part = pl.ds(g * block, block)
        return pltpu.make_async_copy(field_hbm.at[part], field.at[part], field_sems.at[g])

    got = load([(table_hbm, table), (perm_hbm, perm)], in_sems)
    for g in range(CH // block):
        part_copy(g).start()
    got[0].wait()

    def step(g, carry):
        part_copy(g).wait()
        cells = field[pl.ds(g * block, block)].reshape(block * XY, ZT)
        coef = dot(cells, table[...]).astype(BF)
        for c in range(block):
            flat[pl.ds(g * block + c, 1)] = coef[c * XY : (c + 1) * XY].T[None]
        return carry

    lax.fori_loop(0, CH // block, step, 0)
    got[1].wait()
    pack(flat, perm, stage, out_ref, sems)


def plane_stage(field, table, perm):
    return call(
        first_kernel,
        jax.ShapeDtypeStruct((MODES * 2 * CH, XY), BF),
        limit=60,
        in_specs=[HBM] * 3,
        out_specs=HBM,
        scratch_shapes=[
            pltpu.VMEM((CH, XY, ZT), BF),
            pltpu.VMEM((ZT, PAIRS), BF),
            pltpu.VMEM(perm.shape, BF),
            pltpu.VMEM((CH, PAIRS, XY), BF),
            pltpu.VMEM((MODES * 2 * CH, XY), BF),
            pltpu.SemaphoreType.DMA((2,)),
            pltpu.SemaphoreType.DMA((5,)),
            pltpu.SemaphoreType.DMA((8,)),
        ],
    )(field, table, perm)


def mode_tables():
    tables = [x_table(), y_table(), y_table().T, spread_table(), spread_table().T]
    return np.concatenate(
        [t[:, c : c + 256] for t in tables for c in range(0, t.shape[1], 256)], 0
    )


def table_scratch():
    shapes = [(512, 1024), (2048, 256), (256, 2048), (512, 512), (512, 512)]
    return [pltpu.VMEM(shape, BF) for shape in shapes]


def table_pairs(tables_hbm, targets):
    groups = []
    row = 0
    for target in targets:
        group = []
        for c in range(0, target.shape[1], 256):
            rows = target.shape[0]
            group.append((tables_hbm.at[pl.ds(row, rows)], target.at[:, pl.ds(c, 256)]))
            row += rows
        groups.append(group)
    return groups


def tail_tables():
    inverse = plane_tables()[1].astype(np.float32)
    blocks = np.concatenate(np.split(inverse.T, 4), 1)
    perms = np.zeros((512, 1024), np.float32)
    perms[:320, :320] = pack_table(40).T
    perms[:320, 384:704] = pack_table(40)
    return np.concatenate([inverse, blocks, perms], 0)


def tail_pairs(tables_hbm, perm_ref, inv_ref, back_ref, pack_ref):
    perms = [(tables_hbm.at[pl.ds(512, 320), pl.ds(c, 384)], t) for c, t in ((0, perm_ref), (384, pack_ref))]
    blocks = [
        (tables_hbm.at[pl.ds(256, 256), pl.ds(256 * n, 256)], back_ref.at[pl.ds(256 * n, 256)])
        for n in range(4)
    ]
    return [perms[0], (tables_hbm.at[pl.ds(0, 256)], inv_ref)] + blocks + [perms[1]]


def last_tables():
    forward = plane_tables()[0].astype(np.float32).T
    folds = fold_table().reshape(48, 48)
    rest = np.zeros((768, 1024), np.float32)
    rest[:320, :384] = pack_table(48).T
    rest[320:368, :48] = folds
    return np.concatenate([forward, rest], 0)


def last_pairs(tables_hbm, perm_ref, table_ref, fold_ref):
    return [
        (tables_hbm.at[pl.ds(256, 320), pl.ds(0, 384)], perm_ref),
        (tables_hbm.at[pl.ds(0, 256)], table_ref),
        (tables_hbm.at[pl.ds(576, 48), pl.ds(0, 128)], fold_ref),
    ]


def ready(waits, n):
    for copy in waits[n]:
        copy.wait()


def modes_in(msg_ref, x_ref, y_ref, spread_ref, scale, waits):
    rows = [
        jnp.concatenate([msg_ref[j, :, hi].reshape(GY * 8, XY) for j in range(GX)], 1)
        for hi in range(HI)
    ]
    ready(waits, 0)
    after_x = dot(x_ref[...], jnp.concatenate(rows, 0), ((1,), (1,))).astype(BF)
    left = jnp.concatenate(
        [
            jnp.concatenate(
                [after_x[s * MX : (s + 1) * MX, hi * 128 : (hi + 1) * 128] for s in range(2 * LY)], 1
            )
            for hi in range(HI)
        ],
        0,
    )
    ready(waits, 1)
    after_y = dot(left, y_ref[...]) * scale
    grouped = jnp.concatenate(
        [
            jnp.concatenate(
                [
                    after_y[hi * MX + 8 * low : hi * MX + 8 * low + 8, t * 128 : (t + 1) * 128]
                    for low in range(4)
                ],
                1,
            )
            for t in range(2)
            for hi in range(HI)
        ],
        0,
    ).astype(BF)
    ready(waits, 3)
    spread = dot(grouped, spread_ref[...])
    found = {}
    for t in range(2):
        for hi in range(HI):
            for c in range(4):
                at = 4 * t + c
                row = (t * HI + hi) * 8
                found[hi * 4 + at // 2, at % 2] = spread[row : row + 8, c * 128 : (c + 1) * 128]
    return found


def modes_out(found, x_ref, y_back_ref, gather_ref, stage, out_ref, sems, waits):
    rows = []
    for t in range(2):
        for hi in range(HI):
            tiles = []
            for c in range(4):
                at = 4 * t + c
                tiles.append(found[hi * 4 + at // 2, at % 2])
            rows.append(jnp.concatenate(tiles, 1))
    ready(waits, 4)
    gathered = dot(jnp.concatenate(rows, 0).astype(BF), gather_ref[...])
    grouped = jnp.concatenate(
        [
            jnp.concatenate(
                [
                    gathered[(t * HI + hi) * 8 : (t * HI + hi) * 8 + 8, low * 128 : (low + 1) * 128]
                    for t in range(2)
                ],
                1,
            )
            for hi in range(HI)
            for low in range(4)
        ],
        0,
    ).astype(BF)
    ready(waits, 2)
    after_y = dot(grouped, y_back_ref[...]).astype(BF)
    left = jnp.concatenate(
        [
            jnp.concatenate(
                [
                    after_y[hi * MX : (hi + 1) * MX, s * 128 : (s + 1) * 128]
                    for hi in range(HI)
                ],
                1,
            )
            for s in range(2 * LY)
        ],
        0,
    )
    turned = left.T
    sent = []
    for j in range(0, GX, 2):
        after_x = dot(turned, x_ref[:, j * XY : (j + 2) * XY]).astype(BF)
        for e in range(2):
            for hi in range(HI):
                block = after_x[hi * 128 : (hi + 1) * 128, e * XY : (e + 1) * XY]
                stage[j + e, :, hi] = block.reshape(GY, 8, XY)
        part = pl.ds(j, 2)
        sent.append(pltpu.make_async_copy(stage.at[part], out_ref.at[part], sems.at[j // 2]))
        sent[-1].start()
    for copy in sent:
        copy.wait()


def mode_loads(tables_hbm, w_hbm, tables, w_ref, sems):
    groups = table_pairs(tables_hbm, tables)
    order = [groups[0], groups[1], groups[3], [(w_hbm, w_ref)], groups[4], groups[2]]
    moved = load([pair for group in order for pair in group], sems)
    split = []
    for group in order:
        split.append(moved[: len(group)])
        moved = moved[len(group) :]
    return [split[0], split[1], split[5], split[2], split[4]], split[3]


def mix_kernel(msg_ref, w_hbm, tables_hbm, out_ref, spec_ref, *scratch):
    x_ref, y_ref, y_back_ref, spread_ref, gather_ref, w_ref, stage, keep, mixed, in_sems, sems = scratch
    waits, weights = mode_loads(tables_hbm, w_hbm, scratch[:5], w_ref, in_sems)
    spec = modes_in(msg_ref, x_ref, y_ref, spread_ref, 1.0, waits)
    for i in range(CH):
        for r in range(2):
            keep[i, r] = spec[i, r]
    kept = pltpu.make_async_copy(keep, spec_ref.at[0], sems.at[4])
    kept.start()
    weights[0].wait()

    def step(o, carry):
        real = jnp.zeros((8, 128), F32)
        imag = jnp.zeros((8, 128), F32)
        for i in range(CH):
            w_real = w_ref[0, i, o].astype(F32)
            w_imag = w_ref[1, i, o].astype(F32)
            real += w_real * keep[i, 0] - w_imag * keep[i, 1]
            imag += w_real * keep[i, 1] + w_imag * keep[i, 0]
        mixed[o, 0] = 4.0 * real
        mixed[o, 1] = 4.0 * imag
        return carry

    lax.fori_loop(0, CH, step, 0)
    modes_out(mixed, x_ref, y_back_ref, gather_ref, stage, out_ref, sems, waits)
    kept.wait()


def mix_back_kernel(msg_ref, w_hbm, tables_hbm, sums_ref, out_ref, back_ref, *scratch):
    x_ref, y_ref, y_back_ref, spread_ref, gather_ref, w_ref, stage, keep, mixed, in_sems, sems = scratch
    waits, weights = mode_loads(tables_hbm, w_hbm, scratch[:5], w_ref, in_sems)
    for j in range(GX):
        stage[j, :, HI] = jnp.broadcast_to(sums_ref[...][None], (GY, 8, XY))
    back = modes_in(msg_ref, x_ref, y_ref, spread_ref, 4.0, waits)
    for i in range(CH):
        for r in range(2):
            keep[i, r] = back[i, r]
    kept = pltpu.make_async_copy(keep, back_ref.at[0], sems.at[4])
    kept.start()
    weights[0].wait()

    def step(i, carry):
        real = jnp.zeros((8, 128), F32)
        imag = jnp.zeros((8, 128), F32)
        for o in range(CH):
            w_real = w_ref[0, i, o].astype(F32)
            w_imag = w_ref[1, i, o].astype(F32)
            real += w_real * keep[o, 0] + w_imag * keep[o, 1]
            imag += w_real * keep[o, 1] - w_imag * keep[o, 0]
        mixed[i, 0] = real
        mixed[i, 1] = imag
        return carry

    lax.fori_loop(0, CH, step, 0)
    modes_out(mixed, x_ref, y_back_ref, gather_ref, stage, out_ref, sems, waits)
    kept.wait()


def outer_kernel(spec_hbm, back_hbm, grad_ref, spec_ref, back_ref, sems):
    for copy in load([(spec_hbm.at[0], spec_ref), (back_hbm.at[0], back_ref)], sems):
        copy.wait()

    def step(i, carry):
        in_real = spec_ref[i, 0]
        in_imag = spec_ref[i, 1]
        for o in range(CH):
            real = back_ref[o, 0]
            imag = back_ref[o, 1]
            grad_ref[0, i, o] = (in_real * real + in_imag * imag).astype(BF)
            grad_ref[1, i, o] = (in_real * imag - in_imag * real).astype(BF)
        return carry

    lax.fori_loop(0, CH, step, 0)


def bypass_kernel(after_hbm, cells_ref, mix_ref, bias_ref, out_ref):
    for e in range(cells_ref.shape[1]):
        cells = cells_ref[:, e].reshape(CH * LY, ZT)
        total = dot(mix_ref[...], cells) + bias_ref[...]
        out_ref[:, e] = total.reshape(CH, LY, ZT).astype(BF)


def tail_kernel(
    msg_ref, bypass_hbm, cot_hbm, tables_hbm, out_ref, grad_out_ref, coef_ref,
    bypass_ref, cot_ref, inv_ref, back_ref, perm_ref, pack_ref,
    flat, coef, back_coef, stage, out_stage, grad_ref,
    in_sems, bypass_sems, cot_sems, sems, grad_sems, coef_sems,
):
    cells = 16
    rows = CH * cells
    root = math.sqrt(2.0 / math.pi)
    got = load(tail_pairs(tables_hbm, perm_ref, inv_ref, back_ref, pack_ref), in_sems)

    def part(g):
        return pl.ds(pl.multiple_of(g * cells, cells), cells)

    def bypass_copy(g):
        return pltpu.make_async_copy(bypass_hbm.at[:, part(g)], bypass_ref.at[:, part(g)], bypass_sems.at[g])

    def cot_copy(g):
        return pltpu.make_async_copy(cot_hbm.at[:, part(g)], cot_ref.at[:, part(g)], cot_sems.at[g])

    def out_copy(g):
        return pltpu.make_async_copy(out_stage.at[g], out_ref.at[:, part(g)], sems.at[g])

    def grad_copy(g):
        return pltpu.make_async_copy(grad_ref.at[:, part(g)], grad_out_ref.at[:, part(g)], grad_sems.at[g])

    for g in range(XY // cells):
        bypass_copy(g).start()
        cot_copy(g).start()
    got[0].wait()
    unpack(msg_ref, perm_ref, 2 * CH, flat, coef)
    for copy in got[1:]:
        copy.wait()

    def step(g, carry):
        bypass_copy(g).wait()
        cot_copy(g).wait()
        left = coef[:, part(g)].reshape(rows, PAIRS)
        back = jnp.zeros((rows, PAIRS), F32)
        for z in range(0, ZT, LANES):
            at = slice(z, z + LANES)
            bypass = bypass_ref[:, part(g), at].reshape(rows, LANES).astype(F32)
            pre = dot(left, inv_ref[:, at]) + bypass
            cot = cot_ref[:, part(g), at].reshape(rows, LANES).astype(F32)
            square = pre * pre
            bend = jnp.tanh(pre * (root + (root * 0.044715) * square))
            half = 0.5 + 0.5 * bend
            out_stage[g, :, :, at] = (pre * half).astype(BF).reshape(CH, cells, LANES)
            rise = pre * (2.0 * root + (6.0 * root * 0.044715) * square)
            grad = (cot * (half * (1.0 + rise * (1.0 - half)))).astype(BF)
            grad_ref[:, part(g), at] = grad.reshape(CH, cells, LANES)
            back += dot(grad, back_ref[at])
        back_coef[:, part(g)] = back.astype(BF).reshape(CH, cells, PAIRS)
        out_copy(g).start()
        grad_copy(g).start()
        return carry

    def turn(n, carry):
        for e in range(4):
            ch = n * 4 + e
            flat[pl.ds(ch, 1)] = back_coef[ch].T[None]
        return carry

    def drain(g, carry):
        out_copy(g).wait()
        grad_copy(g).wait()
        return carry

    lax.fori_loop(0, XY // cells, step, 0, unroll=U[3])
    lax.fori_loop(0, CH // 4, turn, 0, unroll=U[2])
    pack(flat, pack_ref, stage, coef_ref, coef_sems)
    lax.fori_loop(0, XY // cells, drain, 0)


def sums_kernel(field_hbm, grad_hbm, fold_ref, sums_ref, field_ref, grad_ref, weight_sum, sems):
    for copy in load([(field_hbm, field_ref), (grad_hbm, grad_ref)], sems):
        copy.wait()
    weight_sum[...] = jnp.zeros_like(weight_sum)

    def step(u, carry):
        field = field_ref[:, pl.ds(u, 1)].reshape(CH * LY, ZT)
        grad = grad_ref[:, pl.ds(u, 1)].reshape(CH * LY, ZT)
        ones = jnp.concatenate([field, jnp.ones((16, ZT), BF)], 0)
        weight_sum[...] += dot(ones, grad, ((1,), (1,)))
        return carry

    lax.fori_loop(0, LX, step, 0)
    summed = weight_sum[...]
    rows = lax.broadcasted_iota(jnp.int32, summed.shape, 0)
    lanes = lax.broadcasted_iota(jnp.int32, summed.shape, 1)
    keep = (rows >= CH * LY) | (rows % LY == lanes % LY)
    by_row = jnp.where(keep, summed, 0.0).reshape(CH + 2, LY, CH * LY)
    by_row = jnp.concatenate(
        [jnp.sum(by_row[:CH], 1), by_row[CH, :1], jnp.zeros((3, CH * LY), F32)], 0
    )
    at = lax.broadcasted_iota(jnp.int32, (CH * LY, 128), 0) // LY
    to = lax.broadcasted_iota(jnp.int32, (CH * LY, 128), 1)
    gather = jnp.where(at == to, 1.0, 0.0)
    full = lax.dot_general(
        by_row, gather, (((1,), (0,)), ((), ())),
        precision=lax.Precision.HIGHEST, preferred_element_type=F32,
    )
    high = full.astype(BF)
    low = (full - high.astype(F32)).astype(BF)
    both = jnp.concatenate([high.astype(F32), low.astype(F32)], 0).astype(BF)
    folded = jnp.zeros((8, 128), F32)
    for s in range(6):
        folded += pltpu.roll(dot(fold_ref[s], both), CH * s, 1)
    sums_ref[...] = folded.astype(BF)


def last_kernel(
    msg_ref, bypass_hbm, tables_hbm, out_ref, weight_ref, bias_ref,
    bypass_ref, table_ref, perm_ref, fold_ref, flat, coef, out_stage, in_sems, bypass_sems, sems,
):
    cells = 16
    rows = CH * cells
    got = load(last_pairs(tables_hbm, perm_ref, table_ref, fold_ref), in_sems)

    def part(g):
        return pl.ds(pl.multiple_of(g * cells, cells), cells)

    def bypass_copy(g):
        return pltpu.make_async_copy(bypass_hbm.at[:, part(g)], bypass_ref.at[:, part(g)], bypass_sems.at[g])

    def out_copy(g):
        return pltpu.make_async_copy(out_stage.at[g], out_ref.at[:, part(g)], sems.at[g])

    for g in range(XY // cells):
        bypass_copy(g).start()
    got[0].wait()
    unpack(msg_ref, perm_ref, 48, flat, coef)
    for copy in got[1:]:
        copy.wait()

    def step(g, carry):
        bypass_copy(g).wait()
        left = coef[:, part(g)].reshape(rows, PAIRS)
        for z in range(0, ZT, LANES):
            at = slice(z, z + LANES)
            bypass = bypass_ref[:, part(g), at].reshape(rows, LANES).astype(F32)
            total = dot(left, table_ref[:, at]) + bypass
            out_stage[g, :, :, at] = total.astype(BF).reshape(CH, cells, LANES)
        out_copy(g).start()
        return carry

    lax.fori_loop(0, XY // cells, step, 0, unroll=U[3])

    def add(n, total):
        for e in range(8):
            at = pl.multiple_of((n * 8 + e) * 48 + 40, 8)
            total += msg_ref[pl.ds(at, 8)].astype(F32)
        return total

    summed = lax.fori_loop(0, MODES // 8, add, jnp.zeros((8, 128), F32))
    at = lax.broadcasted_iota(jnp.int32, (8, 128), 1)
    full = jnp.zeros((48, 128), F32)
    for s in range(6):
        own = jnp.where(at < CH, pltpu.roll(summed, (128 - CH * s) % 128, 1), 0.0)
        full += lax.dot_general(
            fold_ref[8 * s : 8 * s + 8, :48].astype(F32), own, (((0,), (0,)), ((), ())),
            precision=lax.Precision.HIGHEST, preferred_element_type=F32,
        )
    full = (full[:24] + full[24:]) * (1.0 / math.sqrt(NX * NY * ZT))
    weight_ref[...] = full[:CH, :CH]
    bias_ref[...] = full[CH : CH + 1, :CH]

    def drain(g, carry):
        out_copy(g).wait()
        return carry

    lax.fori_loop(0, XY // cells, drain, 0)


def exchange(messages):
    return lax.all_to_all(messages, AXES, split_axis=0, concat_axis=0, tiled=True)


DMA = pltpu.SemaphoreType.DMA
GRID = (CH, LX, LY, ZT)
MODE = (CH, 2, 8, 128)
TILES = (GX, GY, HI, 8, XY)
WIDE = (GX, GY, HI + 1, 8, XY)
MESSAGES = (MODES * 2 * CH, XY)
WEIGHT = (2, CH, CH, 8, 128)
MIX = (CH * LY, CH * LY)
FLOPS = 2 * CH * XY * ZT * PAIRS
FLAT = pltpu.VMEM((CH, PAIRS, XY), BF)
COEF = pltpu.VMEM((CH, XY, PAIRS), BF)
FLAT_GRID = (CH, XY, ZT)
CELLS = pltpu.VMEM(FLAT_GRID, BF)
OUT_STAGE = pltpu.VMEM((XY // 16, CH, 16, ZT), BF)
SLOTS = 13


def shaped(shape, kind=BF):
    return jax.ShapeDtypeStruct(shape, kind)


def mode_scratch(shape):
    kept = [pltpu.VMEM(WEIGHT, BF), pltpu.VMEM(shape, BF), pltpu.VMEM(MODE, F32), pltpu.VMEM(MODE, F32)]
    return table_scratch() + kept + [DMA((18,)), DMA((5,))]


def mix_stage(messages, weight, tables):
    return call(
        mix_kernel,
        (shaped(TILES), shaped((SLOTS, *MODE), F32)),
        limit=LIMITS[0],
        in_specs=[VMEM, HBM, HBM],
        out_specs=[HBM, HBM],
        scratch_shapes=mode_scratch(TILES),
    )(messages.reshape(TILES), weight, tables)


def bypass_stage(after, cells, mix, bias):
    block = pl.BlockSpec((CH, 2, LY, ZT), lambda g: (0, g, 0, 0))
    return call(
        bypass_kernel,
        shaped(GRID),
        limit=60,
        cost=(FLOPS, 2 * 5 * MIB),
        grid=(LX // 2,),
        in_specs=[HBM, block, pl.BlockSpec(MIX, lambda g: (0, 0)), pl.BlockSpec((CH * LY, 1), lambda g: (0, 0))],
        out_specs=block,
    )(after, cells, mix, bias).reshape(CH, XY, ZT)


def tail_stage(messages, bypass, cotangent, tables):
    perm = pltpu.VMEM((320, 384), BF)
    return call(
        tail_kernel,
        (shaped(FLAT_GRID), shaped(FLAT_GRID), shaped(MESSAGES)),
        limit=LIMITS[1],
        cost=(2 * FLOPS, 8 * 5 * MIB),
        in_specs=[VMEM] + [HBM] * 3,
        out_specs=[HBM, HBM, HBM],
        scratch_shapes=[
            CELLS, CELLS, pltpu.VMEM((PAIRS, ZT), BF), pltpu.VMEM((ZT, PAIRS), BF), perm, perm,
            FLAT, COEF, COEF, pltpu.VMEM(MESSAGES, BF), OUT_STAGE, CELLS,
            DMA((7,)), DMA((8,)), DMA((8,)), DMA((8,)), DMA((8,)), DMA((8,)),
        ],
    )(messages.reshape(MESSAGES), bypass, cotangent, tables)


def sums_stage(field, grad_pre, folds):
    return call(
        sums_kernel,
        shaped((8, 128)),
        limit=60,
        cost=(FLOPS, 2 * 5 * MIB),
        in_specs=[HBM, HBM, VMEM],
        out_specs=VMEM,
        scratch_shapes=[pltpu.VMEM(GRID, BF)] * 2 + [pltpu.VMEM((CH * LY + 16, CH * LY), F32), DMA((2,))],
    )(field, grad_pre, folds)


def mix_back_stage(messages, weight, tables, sums):
    return call(
        mix_back_kernel,
        (shaped(WIDE), shaped((SLOTS, *MODE), F32)),
        limit=LIMITS[2],
        in_specs=[VMEM, HBM, HBM, VMEM],
        out_specs=[HBM, HBM],
        scratch_shapes=mode_scratch(WIDE),
    )(messages.reshape(TILES), weight, tables, sums)


def outer_stage(spec, modes_back):
    return call(
        outer_kernel,
        shaped(WEIGHT),
        limit=60,
        cost=(8 * CH * CH * 1024, 2 * MIB),
        in_specs=[HBM, HBM],
        scratch_shapes=[pltpu.VMEM(MODE, F32), pltpu.VMEM(MODE, F32), DMA((2,))],
    )(spec, modes_back)


def last_stage(messages, bypass, tables):
    return call(
        last_kernel,
        (shaped(FLAT_GRID), shaped((CH, CH), F32), shaped((1, CH), F32)),
        limit=LIMITS[3],
        cost=(FLOPS, 2 * 5 * MIB),
        in_specs=[VMEM, HBM, HBM],
        out_specs=[HBM, VMEM, VMEM],
        scratch_shapes=[
            CELLS, pltpu.VMEM((PAIRS, ZT), BF), pltpu.VMEM((320, 384), BF), pltpu.VMEM((48, 128), BF),
            FLAT, COEF, OUT_STAGE, DMA((3,)), DMA((8,)), DMA((8,)),
        ],
    )(messages.reshape(MODES * 48, XY), bypass, tables)


def local(field, spectral_weight, bypass_weight, bypass_bias, cotangent):
    eye = jnp.eye(LY, dtype=BF)
    mix_in = jnp.kron(bypass_weight, eye)
    mix_out = jnp.kron(bypass_weight.T, eye)
    bias = jnp.repeat(bypass_bias, LY)[:, None]
    tables = const(mode_tables())
    weight = spectral_weight.reshape(WEIGHT)

    plane = plane_stage(field.reshape(FLAT_GRID), const(plane_tables()[0]), const(pack_table(40)))
    arrived = exchange(plane.reshape(MODES, 2 * CH, XY))
    bypass = bypass_stage(plane, field, mix_out, bias)
    sent, spec = mix_stage(arrived, weight, tables)
    arrived = exchange(sent.reshape(MODES, 2 * CH, XY))
    out_field, grad_pre, back_coef = tail_stage(
        arrived, bypass, cotangent.reshape(FLAT_GRID), const(tail_tables())
    )
    grad_pre = grad_pre.reshape(GRID)
    arrived = exchange(back_coef.reshape(MODES, 2 * CH, XY))
    sums = sums_stage(field, grad_pre, const(fold_table()))
    sent, modes_back = mix_back_stage(arrived, weight, tables, sums)
    arrived = exchange(sent.reshape(MODES, 48, XY))
    bypass = bypass_stage(back_coef, grad_pre, mix_in, jnp.zeros_like(bias))
    spectral_grad = outer_stage(spec, modes_back).reshape(spectral_weight.shape)
    field_grad, weight_grad, bias_grad = last_stage(arrived, bypass, const(last_tables()))
    return (
        out_field.reshape(GRID), field_grad.reshape(GRID), spectral_grad, weight_grad, bias_grad.reshape(CH),
    )


def solution(mesh):
    in_specs = (
        P(None, "gx", "gy", None),
        P(None, AXES, None, None, None),
        P(),
        P(),
        P(None, "gx", "gy", None),
    )
    out_specs = (
        P(None, "gx", "gy", None),
        P(None, "gx", "gy", None),
        P(None, AXES, None, None, None),
        P(),
        P(),
    )
    return jax.shard_map(local, mesh=mesh, in_specs=in_specs, out_specs=out_specs, check_vma=False)
```

time: 172 us -> 160 us (0.930)
  Pallas kernels: 43.3 us -> 71.5 us
  blocking collectives: 26.8 us -> 0 us
  local copies, waits for them, and re-layouts: 27 us -> 15.8 us
  waiting for transfers between devices: 50.7 us -> 45.3 us
  starting transfers between devices: 20.7 us -> 25.3 us
    pallas_call x5 -> x9, Pallas kernels: 43.3 us -> 71.5 us  [the longest x2 16.3 us: bypass_stage(): call(bypass_kernel, shaped(GRID), limit=60, cost=(FLOPS, 2 * 5 * MIB), gr...]
    all_to_all x1 -> x0, blocking collectives: 26.8 us -> none  [exchange(): lax.all_to_all(messages, AXES, split_axis=0, concat_axis=0, tiled=True)]
    unnamed x38 -> x6, local copies, waits for them, and re-layouts: 10 us -> 0.69 us
    all_to_all x3 -> x4, waiting for transfers between devices: 50.7 us -> 45.3 us  [exchange(): lax.all_to_all(messages, AXES, split_axis=0, concat_axis=0, tiled=True)]
    all_to_all x3 -> x4, starting transfers between devices: 20.7 us -> 25.3 us  [exchange(): lax.all_to_all(messages, AXES, split_axis=0, concat_axis=0, tiled=True)]
  transfers between devices with their start and end apart: 3 -> 4, of which waited for: 3 -> 4; matrix products, arithmetic and copies ran while one was open for 10% -> 10% of each run, Pallas kernels for 0% -> 18%
where the time goes in v1:
time: 160 us; the launch traced here: 159 us
  Pallas kernels  71.5 us (45%)
  waiting for transfers between devices  45.3 us (28%)
  starting transfers between devices  25.3 us (16%)
  local copies, waits for them, and re-layouts  15.8 us (10%)
    all_to_all x4, waiting for transfers between devices, exchange(): lax.all_to_all(messages, AXES, split_axis=0, concat_axis=0, tiled=True)  45.3 us
    all_to_all x4, starting transfers between devices, exchange(): lax.all_to_all(messages, AXES, split_axis=0, concat_axis=0, tiled=True)  25.3 us
    pallas_call x2, Pallas kernels, bypass_stage(): call(bypass_kernel, shaped(GRID), limit=60, cost=(FLOPS, 2 * 5 * MIB), gr...  16.3 us
    pallas_call x1, Pallas kernels, tail_stage(): call(tail_kernel, (shaped(FLAT_GRID), shaped(FLAT_GRID), shaped(MESSAGES)...  15.6 us
    pallas_call x1, Pallas kernels, sums_stage(): call(sums_kernel, shaped((8, 128)), limit=60, cost=(FLOPS, 2 * 5 * MIB),...  10.1 us
    pallas_call x1, Pallas kernels, last_stage(): call(last_kernel, (shaped(FLAT_GRID), shaped((CH, CH), F32), shaped((1, C...  7.44 us
    pallas_call x1, Pallas kernels, mix_stage(): call(mix_kernel, (shaped(TILES), shaped((SLOTS, *MODE), F32)), limit=LIMI...  6.59 us
    pallas_call x1, Pallas kernels, mix_back_stage(): call(mix_back_kernel, (shaped(WIDE), shaped((SLOTS, *MODE), F32)), limit=...  6.55 us
  transfers between devices with their start and end apart: 4, of which 4 were waited for; matrix products, arithmetic and copies ran while one was open for 10% of the time, Pallas kernels for 18%

profile of v1, /device:TPU:0, one launch (start us, length us, event | category | flops | bytes accessed | tf_op | source)
XLA Modules:
  0.0 159.0 jit_solution(2610278964254277288)
XLA Ops:
  0.6 6.2 %shard_map.146.after_hbm = bf16[5120,128]{1,0:T(8,128)(2,1)} custom-call(bf16[20,128,1024]{2,1,0:T(8,128)(2,1)} %bitcast.25, bf16[1024,256]{1,0:T(8,128)(2,1)} %constant.15.clone.table_hbm, bf16[320,320]{1,0:T(8,128)(2,1)} %constant.16.clone.perm_hbm), custom_call_target="tpu_custom_call" | custom-call | tf_op jit(solution)/shard_map/pallas_call | solution.py:213
  6.8 11.2 %all-to-all-start = ((bf16[128,40,128]{2,1,0:T(8,128)(2,1)}), bf16[128,40,128]{2,1,0:T(8,128)(2,1)S(1)}, u32[]{:S(2)}, u32[]{:S(2)}) async-start(bf16[128,40,128]{2,1,0:T(8,128)(2,1)} %bitcast.30), calls=%async_computation | async-start | bytes 2621440 | tf_op jit(solution)/shard_map/all_to_all | solution.py:664
  18.0 4.1 %reshape.86 = bf16[2,20,20,8,128]{4,3,0,2,1:T(8,128)(2,1)S(1)} reshape(bf16[2,1,20,20,1024]{4,0,3,2,1:T(2,128)(2,1)} %param.12) | data formatting | bytes 3276800 | tf_op jit(solution)/shard_map/reshape | solution.py:789
  22.0 1.4 copy.19.w_hbm
  23.5 16.3 %all-to-all-done = bf16[128,40,128]{2,1,0:T(8,128)(2,1)S(1)} async-done(((bf16[128,40,128]{2,1,0:T(8,128)(2,1)}), bf16[128,40,128]{2,1,0:T(8,128)(2,1)S(1)}, u32[]{:S(2)}, u32[]{:S(2)}) %all-to-all-start) | async-done | bytes 1310752 | tf_op jit(solution)/shard_map/all_to_all | solution.py:664
  39.7 6.6 %shard_map.147 = (bf16[8,16,5,8,128]{4,3,2,1,0:T(8,128)(2,1)}, f32[13,20,2,8,128]{4,3,2,1,0:T(8,128)}) custom-call(bf16[8,16,5,8,128]{4,3,2,1,0:T(8,128)(2,1)S(1)} %bitcast.22, bf16[2,20,20,8,128]{4,3,2,1,0:T(8,128)(2,1)} %copy.19.w_hbm, bf16[8192,256]{1,0:T(8,128)(2,1)} %constant.14.clone.tables_hbm), custom_call_target="tpu_custom_call" | custom-call | tf_op jit(solution)/shard_map/pallas_call | solution.py:694
  46.3 0.0 copy-start.1
  46.4 0.0 copy-start.2
  46.4 4.7 %all-to-all-start.1 = ((bf16[128,40,128]{2,1,0:T(8,128)(2,1)}), bf16[128,40,128]{2,1,0:T(8,128)(2,1)S(1)}, u32[]{:S(2)}, u32[]{:S(2)}) async-start(bf16[128,40,128]{2,1,0:T(8,128)(2,1)} %bitcast.3), calls=%async_computation.1 | async-start | bytes 2621440 | tf_op jit(solution)/shard_map/all_to_all | solution.py:664
  51.0 0.0 copy-done.1
  51.0 0.1 copy.20
  51.1 0.1 broadcast_in_dim.12
  51.2 0.7 broadcast_in_dim_reshape.4.bias_ref
  51.9 0.2 broadcast_multiply_fusion
  52.1 1.2 mul.44.mix_ref
  53.3 8.1 %shard_map.148 = bf16[20,16,8,1024]{3,2,1,0:T(8,128)(2,1)} custom-call(bf16[5120,128]{1,0:T(8,128)(2,1)} %shard_map.146.after_hbm, bf16[20,16,8,1024]{3,2,1,0:T(8,128)(2,1)} %field_hbm.1, bf16[160,160]{1,0:T(8,128)(2,1)} %mul.44.mix_ref, f32[160,1]{1,0:T(8,128)} %broadcast_in_dim_reshape.4.bias_ref), custom_call_target="tpu_custom_call" | custom-call | flops 1342177280 | bytes 10485760 | tf_op jit(solution)/shard_map/pallas_call | solution.py:706
  61.5 11.3 %all-to-all-done.1 = bf16[128,40,128]{2,1,0:T(8,128)(2,1)S(1)} async-done(((bf16[128,40,128]{2,1,0:T(8,128)(2,1)}), bf16[128,40,128]{2,1,0:T(8,128)(2,1)S(1)}, u32[]{:S(2)}, u32[]{:S(2)}) %all-to-all-start.1) | async-done | bytes 1310752 | tf_op jit(solution)/shard_map/all_to_all | solution.py:664
  72.8 15.6 %shard_map.149 = (bf16[20,128,1024]{2,1,0:T(8,128)(2,1)}, bf16[20,128,1024]{2,1,0:T(8,128)(2,1)}, bf16[5120,128]{1,0:T(8,128)(2,1)}) custom-call(bf16[5120,128]{1,0:T(8,128)(2,1)S(1)} %bitcast.24, bf16[20,128,1024]{2,1,0:T(8,128)(2,1)} %bitcast.29, bf16[20,128,1024]{2,1,0:T(8,128)(2,1)} %bitcast.31, bf16[1024,1024]{1,0:T(8,128)(2,1)} %constant.17.clone.tables_hbm), custom_call_target="tpu_custom_call" | custom-call | flops 2684354560 | bytes 41943040 | tf_op jit(solution)/shard_map/pallas_call | solution.py:719
  88.4 4.8 %all-to-all-start.2 = ((bf16[128,40,128]{2,1,0:T(8,128)(2,1)}), bf16[128,40,128]{2,1,0:T(8,128)(2,1)S(1)}, u32[]{:S(2)}, u32[]{:S(2)}) async-start(bf16[128,40,128]{2,1,0:T(8,128)(2,1)} %bitcast.9), calls=%async_computation.2 | async-start | bytes 2621440 | tf_op jit(solution)/shard_map/all_to_all | solution.py:664
  93.3 10.1 %shard_map.150.sums_ref = bf16[8,128]{1,0:T(8,128)(2,1)} custom-call(bf16[20,16,8,1024]{3,2,1,0:T(8,128)(2,1)} %field_hbm.1, bf16[20,16,8,1024]{3,2,1,0:T(8,128)(2,1)} %bitcast.26, bf16[6,8,48]{2,1,0:T(8,128)(2,1)} %constant.18.clone.fold_ref), custom_call_target="tpu_custom_call" | custom-call | flops 1342177280 | bytes 10485760 | tf_op jit(solution)/shard_map/pallas_call | solution.py:735
  103.3 11.7 %all-to-all-done.2 = bf16[128,40,128]{2,1,0:T(8,128)(2,1)S(1)} async-done(((bf16[128,40,128]{2,1,0:T(8,128)(2,1)}), bf16[128,40,128]{2,1,0:T(8,128)(2,1)S(1)}, u32[]{:S(2)}, u32[]{:S(2)}) %all-to-all-start.2) | async-done | bytes 1310752 | tf_op jit(solution)/shard_map/all_to_all | solution.py:664
  115.0 0.7 copy-done
  115.7 6.6 %shard_map.151 = (bf16[8,16,6,8,128]{4,3,2,1,0:T(8,128)(2,1)}, f32[13,20,2,8,128]{4,3,2,1,0:T(8,128)}) custom-call(bf16[8,16,5,8,128]{4,3,2,1,0:T(8,128)(2,1)S(1)} %bitcast.23, bf16[2,20,20,8,128]{4,3,2,1,0:T(8,128)(2,1)} %copy.19.w_hbm, bf16[8192,256]{1,0:T(8,128)(2,1)} %constant.14.clone.tables_hbm, bf16[8,128]{1,0:T(8,128)(2,1)S(1)} %copy-done), custom_call_target="tpu_custom_call" | custom-call | tf_op jit(solution)/shard_map/pallas_call | solution.py:747
  122.3 4.7 %all-to-all-start.3 = ((bf16[128,48,128]{2,1,0:T(8,128)(2,1)}), bf16[128,48,128]{2,1,0:T(8,128)(2,1)S(1)}, u32[]{:S(2)}, u32[]{:S(2)}) async-start(bf16[128,48,128]{2,1,0:T(8,128)(2,1)} %bitcast.12), calls=%async_computation.3 | async-start | bytes 3145728 | tf_op jit(solution)/shard_map/all_to_all | solution.py:664
  126.9 1.2 mul.47.mix_ref
  128.1 0.6 broadcast_in_dim.13.bias_ref
  128.8 8.2 %shard_map.152 = bf16[20,16,8,1024]{3,2,1,0:T(8,128)(2,1)} custom-call(bf16[5120,128]{1,0:T(8,128)(2,1)} %get-tuple-element.17.after_hbm, bf16[20,16,8,1024]{3,2,1,0:T(8,128)(2,1)} %bitcast.27, bf16[160,160]{1,0:T(8,128)(2,1)} %mul.47.mix_ref, f32[160,1]{1,0:T(8,128)} %broadcast_in_dim.13.bias_ref), custom_call_target="tpu_custom_call" | custom-call | flops 1342177280 | bytes 10485760 | tf_op jit(solution)/shard_map/pallas_call | solution.py:706
  137.0 2.7 %shard_map.154 = bf16[2,20,20,8,128]{4,3,2,1,0:T(8,128)(2,1)} custom-call(f32[13,20,2,8,128]{4,3,2,1,0:T(8,128)} %get-tuple-element.21.spec_hbm, f32[13,20,2,8,128]{4,3,2,1,0:T(8,128)} %get-tuple-element.22.back_hbm), custom_call_target="tpu_custom_call" | custom-call | flops 3276800 | bytes 2097152 | tf_op jit(solution)/shard_map/pallas_call | solution.py:758
  139.7 2.8 %reshape.101 = bf16[2,1,20,20,1024]{4,3,2,0,1:T(8,128)(2,1)S(1)} reshape(bf16[2,20,20,8,128]{4,3,2,1,0:T(8,128)(2,1)} %shard_map.154) | data formatting | bytes 3276800 | tf_op jit(solution)/shard_map/reshape | solution.py:805
  142.5 2.9 %copy.24 = bf16[2,1,20,20,1024]{4,0,3,2,1:T(2,128)(2,1)} copy(bf16[2,1,20,20,1024]{4,3,2,0,1:T(8,128)(2,1)S(1)} %reshape.101) | data formatting | bytes 3276800 | tf_op jit(solution)/shard_map/reshape | solution.py:805
  145.3 6.0 %all-to-all-done.3 = bf16[128,48,128]{2,1,0:T(8,128)(2,1)S(1)} async-done(((bf16[128,48,128]{2,1,0:T(8,128)(2,1)}), bf16[128,48,128]{2,1,0:T(8,128)(2,1)S(1)}, u32[]{:S(2)}, u32[]{:S(2)}) %all-to-all-start.3) | async-done | bytes 1572896 | tf_op jit(solution)/shard_map/all_to_all | solution.py:664
  151.4 7.4 %shard_map.153 = (bf16[20,128,1024]{2,1,0:T(8,128)(2,1)}, f32[20,20]{1,0:T(8,128)}, f32[1,20]{1,0:T(1,128)}) custom-call(bf16[6144,128]{1,0:T(8,128)(2,1)S(1)} %bitcast.21, bf16[20,128,1024]{2,1,0:T(8,128)(2,1)} %bitcast.28, bf16[1024,1024]{1,0:T(8,128)(2,1)} %constant.19.clone.tables_hbm), custom_call_target="tpu_custom_call" | custom-call | flops 1342177280 | bytes 10485760 | tf_op jit(solution)/shard_map/pallas_call | solution.py:769
  (3 shorter events, 0.0 us)
Async XLA Ops:
  6.8 32.9 %all-to-all-start = ((bf16[128,40,128]{2,1,0:T(8,128)(2,1)}), bf16[128,40,128]{2,1,0:T(8,128)(2,1)S(1)}, u32[]{:S(2)}, u32[]{:S(2)}) async-start(bf16[128,40,128]{2,1,0:T(8,128)(2,1)} %bitcast.30), calls=%async_computation | async-start | bytes 2621440 | tf_op jit(solution)/shard_map/all_to_all | solution.py:664
  46.3 4.7 %copy-start.1 = (bf16[20,20]{1,0:T(8,128)(2,1)S(1)}, bf16[20,20]{1,0:T(8,128)(2,1)}, u32[]{:S(2)}) copy-start(bf16[20,20]{1,0:T(8,128)(2,1)} %param.13) | copy-start | bytes 2404
  46.4 4.8 %copy-start.2 = (f32[20]{0:T(128)S(1)}, f32[20]{0:T(128)}, u32[]{:S(2)}) copy-start(f32[20]{0:T(128)} %param.14) | copy-start | bytes 244
  46.4 26.4 %all-to-all-start.1 = ((bf16[128,40,128]{2,1,0:T(8,128)(2,1)}), bf16[128,40,128]{2,1,0:T(8,128)(2,1)S(1)}, u32[]{:S(2)}, u32[]{:S(2)}) async-start(bf16[128,40,128]{2,1,0:T(8,128)(2,1)} %bitcast.3), calls=%async_computation.1 | async-start | bytes 2621440 | tf_op jit(solution)/shard_map/all_to_all | solution.py:664
  88.4 26.6 %all-to-all-start.2 = ((bf16[128,40,128]{2,1,0:T(8,128)(2,1)}), bf16[128,40,128]{2,1,0:T(8,128)(2,1)S(1)}, u32[]{:S(2)}, u32[]{:S(2)}) async-start(bf16[128,40,128]{2,1,0:T(8,128)(2,1)} %bitcast.9), calls=%async_computation.2 | async-start | bytes 2621440 | tf_op jit(solution)/shard_map/all_to_all | solution.py:664
  115.0 0.7 copy-start
  122.3 29.1 %all-to-all-start.3 = ((bf16[128,48,128]{2,1,0:T(8,128)(2,1)}), bf16[128,48,128]{2,1,0:T(8,128)(2,1)S(1)}, u32[]{:S(2)}, u32[]{:S(2)}) async-start(bf16[128,48,128]{2,1,0:T(8,128)(2,1)} %bitcast.12), calls=%async_computation.3 | async-start | bytes 3145728 | tf_op jit(solution)/shard_map/all_to_all | solution.py:664

commit v2 on v1

--- a/solution.py
+++ b/solution.py
@@ -405,7 +405,7 @@
 
 
 def mix_kernel(msg_ref, w_hbm, tables_hbm, out_ref, spec_ref, *scratch):
-    x_ref, y_ref, y_back_ref, spread_ref, gather_ref, w_ref, stage, keep, mixed, in_sems, sems = scratch
+    x_ref, y_ref, y_back_ref, spread_ref, gather_ref, w_ref, stage, keep, mixed, unused, in_sems, sems = scratch
     waits, weights = mode_loads(tables_hbm, w_hbm, scratch[:5], w_ref, in_sems)
     spec = modes_in(msg_ref, x_ref, y_ref, spread_ref, 1.0, waits)
     for i in range(CH):
@@ -432,12 +432,15 @@
     kept.wait()
 
 
-def mix_back_kernel(msg_ref, w_hbm, tables_hbm, sums_ref, out_ref, back_ref, *scratch):
-    x_ref, y_ref, y_back_ref, spread_ref, gather_ref, w_ref, stage, keep, mixed, in_sems, sems = scratch
+def mix_back_kernel(msg_ref, w_hbm, tables_hbm, sums_hbm, out_ref, back_ref, *scratch):
+    x_ref, y_ref, y_back_ref, spread_ref, gather_ref, w_ref, stage, keep, mixed, sums_ref, in_sems, sems = scratch
     waits, weights = mode_loads(tables_hbm, w_hbm, scratch[:5], w_ref, in_sems)
+    fetched = pltpu.make_async_copy(sums_hbm.at[0], sums_ref, sems.at[5])
+    fetched.start()
+    back = modes_in(msg_ref, x_ref, y_ref, spread_ref, 4.0, waits)
+    fetched.wait()
     for j in range(GX):
         stage[j, :, HI] = jnp.broadcast_to(sums_ref[...][None], (GY, 8, XY))
-    back = modes_in(msg_ref, x_ref, y_ref, spread_ref, 4.0, waits)
     for i in range(CH):
         for r in range(2):
             keep[i, r] = back[i, r]
@@ -529,13 +532,15 @@
             at = slice(z, z + LANES)
             bypass = bypass_ref[:, part(g), at].reshape(rows, LANES).astype(F32)
             pre = dot(left, inv_ref[:, at]) + bypass
-            cot = cot_ref[:, part(g), at].reshape(rows, LANES).astype(F32)
+            cot = cot_ref[:, part(g), at].reshape(rows, LANES)
             square = pre * pre
             bend = jnp.tanh(pre * (root + (root * 0.044715) * square))
             half = 0.5 + 0.5 * bend
             out_stage[g, :, :, at] = (pre * half).astype(BF).reshape(CH, cells, LANES)
-            rise = pre * (2.0 * root + (6.0 * root * 0.044715) * square)
-            grad = (cot * (half * (1.0 + rise * (1.0 - half)))).astype(BF)
+            half = half.astype(BF)
+            near = pre.astype(BF)
+            rise = near * (BF(2.0 * root) + BF(6.0 * root * 0.044715) * (near * near))
+            grad = cot * (half * (BF(1.0) + rise * (BF(1.0) - half)))
             grad_ref[:, part(g), at] = grad.reshape(CH, cells, LANES)
             back += dot(grad, back_ref[at])
         back_coef[:, part(g)] = back.astype(BF).reshape(CH, cells, PAIRS)
@@ -560,7 +565,9 @@
     lax.fori_loop(0, XY // cells, drain, 0)
 
 
-def sums_kernel(field_hbm, grad_hbm, fold_ref, sums_ref, field_ref, grad_ref, weight_sum, sems):
+def sums_kernel(
+    field_hbm, grad_hbm, fold_ref, sums_ref, field_ref, grad_ref, weight_sum, folds_ref, sems
+):
     for copy in load([(field_hbm, field_ref), (grad_hbm, grad_ref)], sems):
         copy.wait()
     weight_sum[...] = jnp.zeros_like(weight_sum)
@@ -594,7 +601,10 @@
     folded = jnp.zeros((8, 128), F32)
     for s in range(6):
         folded += pltpu.roll(dot(fold_ref[s], both), CH * s, 1)
-    sums_ref[...] = folded.astype(BF)
+    folds_ref[...] = folded.astype(BF)
+    sent = pltpu.make_async_copy(folds_ref, sums_ref.at[0], sems.at[0])
+    sent.start()
+    sent.wait()
 
 
 def last_kernel(
@@ -687,7 +697,7 @@
 
 def mode_scratch(shape):
     kept = [pltpu.VMEM(WEIGHT, BF), pltpu.VMEM(shape, BF), pltpu.VMEM(MODE, F32), pltpu.VMEM(MODE, F32)]
-    return table_scratch() + kept + [DMA((18,)), DMA((5,))]
+    return table_scratch() + kept + [pltpu.VMEM((8, 128), BF), DMA((18,)), DMA((6,))]
 
 
 def mix_stage(messages, weight, tables):
@@ -734,12 +744,13 @@
 def sums_stage(field, grad_pre, folds):
     return call(
         sums_kernel,
-        shaped((8, 128)),
+        shaped((1280, 8, 128)),
         limit=60,
         cost=(FLOPS, 2 * 5 * MIB),
         in_specs=[HBM, HBM, VMEM],
-        out_specs=VMEM,
-        scratch_shapes=[pltpu.VMEM(GRID, BF)] * 2 + [pltpu.VMEM((CH * LY + 16, CH * LY), F32), DMA((2,))],
+        out_specs=HBM,
+        scratch_shapes=[pltpu.VMEM(GRID, BF)] * 2
+        + [pltpu.VMEM((CH * LY + 16, CH * LY), F32), pltpu.VMEM((8, 128), BF), DMA((2,))],
     )(field, grad_pre, folds)
 
 
@@ -748,7 +759,7 @@
         mix_back_kernel,
         (shaped(WIDE), shaped((SLOTS, *MODE), F32)),
         limit=LIMITS[2],
-        in_specs=[VMEM, HBM, HBM, VMEM],
+        in_specs=[VMEM, HBM, HBM, HBM],
         out_specs=[HBM, HBM],
         scratch_shapes=mode_scratch(WIDE),
     )(messages.reshape(TILES), weight, tables, sums)

time: 160 us -> 158 us (0.988)
  transfers between devices with their start and end apart: 4 -> 4, of which waited for: 4 -> 4; matrix products, arithmetic and copies ran while one was open for 10% -> 10% of each run, Pallas kernels for 18% -> 19%
where the time goes in v2:
time: 158 us; the launch traced here: 157 us
  Pallas kernels  70.6 us (45%)
  waiting for transfers between devices  45 us (28%)
  starting transfers between devices  25.3 us (16%)
  local copies, waits for them, and re-layouts  15.1 us (10%)
    all_to_all x4, waiting for transfers between devices, exchange(): lax.all_to_all(messages, AXES, split_axis=0, concat_axis=0, tiled=True)  45 us
    all_to_all x4, starting transfers between devices, exchange(): lax.all_to_all(messages, AXES, split_axis=0, concat_axis=0, tiled=True)  25.3 us
    pallas_call x2, Pallas kernels, bypass_stage(): call(bypass_kernel, shaped(GRID), limit=60, cost=(FLOPS, 2 * 5 * MIB), gr...  16.4 us
    pallas_call x1, Pallas kernels, tail_stage(): call(tail_kernel, (shaped(FLAT_GRID), shaped(FLAT_GRID), shaped(MESSAGES)...  14.5 us
    pallas_call x1, Pallas kernels, sums_stage(): call(sums_kernel, shaped((1280, 8, 128)), limit=60, cost=(FLOPS, 2 * 5 *...  10.1 us
    pallas_call x1, Pallas kernels, last_stage(): call(last_kernel, (shaped(FLAT_GRID), shaped((CH, CH), F32), shaped((1, C...  7.44 us
    pallas_call x1, Pallas kernels, mix_back_stage(): call(mix_back_kernel, (shaped(WIDE), shaped((SLOTS, *MODE), F32)), limit=...  6.63 us
    pallas_call x1, Pallas kernels, mix_stage(): call(mix_kernel, (shaped(TILES), shaped((SLOTS, *MODE), F32)), limit=LIMI...  6.58 us
  transfers between devices with their start and end apart: 4, of which 4 were waited for; matrix products, arithmetic and copies ran while one was open for 10% of the time, Pallas kernels for 19%

profile of v2, /device:TPU:0, one launch (start us, length us, event | category | flops | bytes accessed | tf_op | source)
XLA Modules:
  0.0 157.1 jit_solution(10439343559160508481)
XLA Ops:
  0.6 6.2 %shard_map.146.after_hbm = bf16[5120,128]{1,0:T(8,128)(2,1)} custom-call(bf16[20,128,1024]{2,1,0:T(8,128)(2,1)} %bitcast.25, bf16[1024,256]{1,0:T(8,128)(2,1)} %constant.15.clone.table_hbm, bf16[320,320]{1,0:T(8,128)(2,1)} %constant.16.clone.perm_hbm), custom_call_target="tpu_custom_call" | custom-call | tf_op jit(solution)/shard_map/pallas_call | solution.py:213
  6.8 11.2 %all-to-all-start = ((bf16[128,40,128]{2,1,0:T(8,128)(2,1)}), bf16[128,40,128]{2,1,0:T(8,128)(2,1)S(1)}, u32[]{:S(2)}, u32[]{:S(2)}) async-start(bf16[128,40,128]{2,1,0:T(8,128)(2,1)} %bitcast.30), calls=%async_computation | async-start | bytes 2621440 | tf_op jit(solution)/shard_map/all_to_all | solution.py:674
  18.0 4.1 %reshape.86 = bf16[2,20,20,8,128]{4,3,0,2,1:T(8,128)(2,1)S(1)} reshape(bf16[2,1,20,20,1024]{4,0,3,2,1:T(2,128)(2,1)} %param.12) | data formatting | bytes 3276800 | tf_op jit(solution)/shard_map/reshape | solution.py:800
  22.0 1.4 copy.19.w_hbm
  23.5 16.3 %all-to-all-done = bf16[128,40,128]{2,1,0:T(8,128)(2,1)S(1)} async-done(((bf16[128,40,128]{2,1,0:T(8,128)(2,1)}), bf16[128,40,128]{2,1,0:T(8,128)(2,1)S(1)}, u32[]{:S(2)}, u32[]{:S(2)}) %all-to-all-start) | async-done | bytes 1310752 | tf_op jit(solution)/shard_map/all_to_all | solution.py:674
  39.7 6.6 %shard_map.147 = (bf16[8,16,5,8,128]{4,3,2,1,0:T(8,128)(2,1)}, f32[13,20,2,8,128]{4,3,2,1,0:T(8,128)}) custom-call(bf16[8,16,5,8,128]{4,3,2,1,0:T(8,128)(2,1)S(1)} %bitcast.23, bf16[2,20,20,8,128]{4,3,2,1,0:T(8,128)(2,1)} %copy.19.w_hbm, bf16[8192,256]{1,0:T(8,128)(2,1)} %constant.14.clone.tables_hbm), custom_call_target="tpu_custom_call" | custom-call | tf_op jit(solution)/shard_map/pallas_call | solution.py:704
  46.3 0.0 copy-start
  46.3 0.0 copy-start.1
  46.4 4.7 %all-to-all-start.1 = ((bf16[128,40,128]{2,1,0:T(8,128)(2,1)}), bf16[128,40,128]{2,1,0:T(8,128)(2,1)S(1)}, u32[]{:S(2)}, u32[]{:S(2)}) async-start(bf16[128,40,128]{2,1,0:T(8,128)(2,1)} %bitcast.3), calls=%async_computation.1 | async-start | bytes 2621440 | tf_op jit(solution)/shard_map/all_to_all | solution.py:674
  51.0 0.0 copy-done
  51.0 0.1 copy.20
  51.1 0.0 copy-done.1
  51.1 0.1 broadcast_in_dim.12
  51.2 0.7 broadcast_in_dim_reshape.4.bias_ref
  51.9 0.2 broadcast_multiply_fusion
  52.1 1.2 mul.44.mix_ref
  53.3 8.1 %shard_map.148 = bf16[20,16,8,1024]{3,2,1,0:T(8,128)(2,1)} custom-call(bf16[5120,128]{1,0:T(8,128)(2,1)} %shard_map.146.after_hbm, bf16[20,16,8,1024]{3,2,1,0:T(8,128)(2,1)} %field_hbm.1, bf16[160,160]{1,0:T(8,128)(2,1)} %mul.44.mix_ref, f32[160,1]{1,0:T(8,128)} %broadcast_in_dim_reshape.4.bias_ref), custom_call_target="tpu_custom_call" | custom-call | flops 1342177280 | bytes 10485760 | tf_op jit(solution)/shard_map/pallas_call | solution.py:716
  61.4 11.3 %all-to-all-done.1 = bf16[128,40,128]{2,1,0:T(8,128)(2,1)S(1)} async-done(((bf16[128,40,128]{2,1,0:T(8,128)(2,1)}), bf16[128,40,128]{2,1,0:T(8,128)(2,1)S(1)}, u32[]{:S(2)}, u32[]{:S(2)}) %all-to-all-start.1) | async-done | bytes 1310752 | tf_op jit(solution)/shard_map/all_to_all | solution.py:674
  72.8 14.5 %shard_map.149 = (bf16[20,128,1024]{2,1,0:T(8,128)(2,1)}, bf16[20,128,1024]{2,1,0:T(8,128)(2,1)}, bf16[5120,128]{1,0:T(8,128)(2,1)}) custom-call(bf16[5120,128]{1,0:T(8,128)(2,1)S(1)} %bitcast.24, bf16[20,128,1024]{2,1,0:T(8,128)(2,1)} %bitcast.29, bf16[20,128,1024]{2,1,0:T(8,128)(2,1)} %bitcast.31, bf16[1024,1024]{1,0:T(8,128)(2,1)} %constant.17.clone.tables_hbm), custom_call_target="tpu_custom_call" | custom-call | flops 2684354560 | bytes 41943040 | tf_op jit(solution)/shard_map/pallas_call | solution.py:729
  87.3 4.8 %all-to-all-start.2 = ((bf16[128,40,128]{2,1,0:T(8,128)(2,1)}), bf16[128,40,128]{2,1,0:T(8,128)(2,1)S(1)}, u32[]{:S(2)}, u32[]{:S(2)}) async-start(bf16[128,40,128]{2,1,0:T(8,128)(2,1)} %bitcast.9), calls=%async_computation.2 | async-start | bytes 2621440 | tf_op jit(solution)/shard_map/all_to_all | solution.py:674
  92.2 10.1 %shard_map.150.sums_hbm = bf16[1280,8,128]{2,1,0:T(8,128)(2,1)} custom-call(bf16[20,16,8,1024]{3,2,1,0:T(8,128)(2,1)} %field_hbm.1, bf16[20,16,8,1024]{3,2,1,0:T(8,128)(2,1)} %bitcast.26, bf16[6,8,48]{2,1,0:T(8,128)(2,1)} %constant.18.clone.fold_ref), custom_call_target="tpu_custom_call" | custom-call | flops 1342177280 | bytes 10485760 | tf_op jit(solution)/shard_map/pallas_call | solution.py:745
  102.3 11.4 %all-to-all-done.2 = bf16[128,40,128]{2,1,0:T(8,128)(2,1)S(1)} async-done(((bf16[128,40,128]{2,1,0:T(8,128)(2,1)}), bf16[128,40,128]{2,1,0:T(8,128)(2,1)S(1)}, u32[]{:S(2)}, u32[]{:S(2)}) %all-to-all-start.2) | async-done | bytes 1310752 | tf_op jit(solution)/shard_map/all_to_all | solution.py:674
  113.8 6.6 %shard_map.151 = (bf16[8,16,6,8,128]{4,3,2,1,0:T(8,128)(2,1)}, f32[13,20,2,8,128]{4,3,2,1,0:T(8,128)}) custom-call(bf16[8,16,5,8,128]{4,3,2,1,0:T(8,128)(2,1)S(1)} %bitcast.22, bf16[2,20,20,8,128]{4,3,2,1,0:T(8,128)(2,1)} %copy.19.w_hbm, bf16[8192,256]{1,0:T(8,128)(2,1)} %constant.14.clone.tables_hbm, bf16[1280,8,128]{2,1,0:T(8,128)(2,1)} %shard_map.150.sums_hbm), custom_call_target="tpu_custom_call" | custom-call | tf_op jit(solution)/shard_map/pallas_call | solution.py:758
  120.4 4.7 %all-to-all-start.3 = ((bf16[128,48,128]{2,1,0:T(8,128)(2,1)}), bf16[128,48,128]{2,1,0:T(8,128)(2,1)S(1)}, u32[]{:S(2)}, u32[]{:S(2)}) async-start(bf16[128,48,128]{2,1,0:T(8,128)(2,1)} %bitcast.12), calls=%async_computation.3 | async-start | bytes 3145728 | tf_op jit(solution)/shard_map/all_to_all | solution.py:674
  125.1 1.2 mul.47.mix_ref
  126.2 0.6 broadcast_in_dim.13.bias_ref
  126.9 8.3 %shard_map.152 = bf16[20,16,8,1024]{3,2,1,0:T(8,128)(2,1)} custom-call(bf16[5120,128]{1,0:T(8,128)(2,1)} %get-tuple-element.17.after_hbm, bf16[20,16,8,1024]{3,2,1,0:T(8,128)(2,1)} %bitcast.27, bf16[160,160]{1,0:T(8,128)(2,1)} %mul.47.mix_ref, f32[160,1]{1,0:T(8,128)} %broadcast_in_dim.13.bias_ref), custom_call_target="tpu_custom_call" | custom-call | flops 1342177280 | bytes 10485760 | tf_op jit(solution)/shard_map/pallas_call | solution.py:716
  135.2 2.7 %shard_map.154 = bf16[2,20,20,8,128]{4,3,2,1,0:T(8,128)(2,1)} custom-call(f32[13,20,2,8,128]{4,3,2,1,0:T(8,128)} %get-tuple-element.21.spec_hbm, f32[13,20,2,8,128]{4,3,2,1,0:T(8,128)} %get-tuple-element.22.back_hbm), custom_call_target="tpu_custom_call" | custom-call | flops 3276800 | bytes 2097152 | tf_op jit(solution)/shard_map/pallas_call | solution.py:769
  137.9 2.8 %reshape.101 = bf16[2,1,20,20,1024]{4,3,2,0,1:T(8,128)(2,1)S(1)} reshape(bf16[2,20,20,8,128]{4,3,2,1,0:T(8,128)(2,1)} %shard_map.154) | data formatting | bytes 3276800 | tf_op jit(solution)/shard_map/reshape | solution.py:816
  140.7 2.9 %copy.24 = bf16[2,1,20,20,1024]{4,0,3,2,1:T(2,128)(2,1)} copy(bf16[2,1,20,20,1024]{4,3,2,0,1:T(8,128)(2,1)S(1)} %reshape.101) | data formatting | bytes 3276800 | tf_op jit(solution)/shard_map/reshape | solution.py:816
  143.6 6.0 %all-to-all-done.3 = bf16[128,48,128]{2,1,0:T(8,128)(2,1)S(1)} async-done(((bf16[128,48,128]{2,1,0:T(8,128)(2,1)}), bf16[128,48,128]{2,1,0:T(8,128)(2,1)S(1)}, u32[]{:S(2)}, u32[]{:S(2)}) %all-to-all-start.3) | async-done | bytes 1572896 | tf_op jit(solution)/shard_map/all_to_all | solution.py:674
  149.5 7.4 %shard_map.153 = (bf16[20,128,1024]{2,1,0:T(8,128)(2,1)}, f32[20,20]{1,0:T(8,128)}, f32[1,20]{1,0:T(1,128)}) custom-call(bf16[6144,128]{1,0:T(8,128)(2,1)S(1)} %bitcast.21, bf16[20,128,1024]{2,1,0:T(8,128)(2,1)} %bitcast.28, bf16[1024,1024]{1,0:T(8,128)(2,1)} %constant.19.clone.tables_hbm), custom_call_target="tpu_custom_call" | custom-call | flops 1342177280 | bytes 10485760 | tf_op jit(solution)/shard_map/pallas_call | solution.py:780
  (1 shorter events, 0.0 us)
Async XLA Ops:
  6.8 32.9 %all-to-all-start = ((bf16[128,40,128]{2,1,0:T(8,128)(2,1)}), bf16[128,40,128]{2,1,0:T(8,128)(2,1)S(1)}, u32[]{:S(2)}, u32[]{:S(2)}) async-start(bf16[128,40,128]{2,1,0:T(8,128)(2,1)} %bitcast.30), calls=%async_computation | async-start | bytes 2621440 | tf_op jit(solution)/shard_map/all_to_all | solution.py:674
  46.3 4.7 %copy-start = (bf16[20,20]{1,0:T(8,128)(2,1)S(1)}, bf16[20,20]{1,0:T(8,128)(2,1)}, u32[]{:S(2)}) copy-start(bf16[20,20]{1,0:T(8,128)(2,1)} %param.13) | copy-start | bytes 2404
  46.3 4.8 %copy-start.1 = (f32[20]{0:T(128)S(1)}, f32[20]{0:T(128)}, u32[]{:S(2)}) copy-start(f32[20]{0:T(128)} %param.14) | copy-start | bytes 244
  46.4 26.4 %all-to-all-start.1 = ((bf16[128,40,128]{2,1,0:T(8,128)(2,1)}), bf16[128,40,128]{2,1,0:T(8,128)(2,1)S(1)}, u32[]{:S(2)}, u32[]{:S(2)}) async-start(bf16[128,40,128]{2,1,0:T(8,128)(2,1)} %bitcast.3), calls=%async_computation.1 | async-start | bytes 2621440 | tf_op jit(solution)/shard_map/all_to_all | solution.py:674
  87.3 26.4 %all-to-all-start.2 = ((bf16[128,40,128]{2,1,0:T(8,128)(2,1)}), bf16[128,40,128]{2,1,0:T(8,128)(2,1)S(1)}, u32[]{:S(2)}, u32[]{:S(2)}) async-start(bf16[128,40,128]{2,1,0:T(8,128)(2,1)} %bitcast.9), calls=%async_computation.2 | async-start | bytes 2621440 | tf_op jit(solution)/shard_map/all_to_all | solution.py:674
  120.4 29.1 %all-to-all-start.3 = ((bf16[128,48,128]{2,1,0:T(8,128)(2,1)}), bf16[128,48,128]{2,1,0:T(8,128)(2,1)S(1)}, u32[]{:S(2)}, u32[]{:S(2)}) async-start(bf16[128,48,128]{2,1,0:T(8,128)(2,1)} %bitcast.12), calls=%async_computation.3 | async-start | bytes 3145728 | tf_op jit(solution)/shard_map/all_to_all | solution.py:674

commit v3 on v2

--- a/solution.py
+++ b/solution.py
@@ -91,12 +91,12 @@
 
 
 def pack_table(rows):
-    table = np.zeros((8, rows, CH, 8, 2), np.float32)
-    for m in range(8):
+    table = np.zeros((4, rows, CH, 4, 2), np.float32)
+    for m in range(4):
         for ch in range(CH):
             for r in range(2):
                 table[m, 2 * ch + r, ch, m, r] = 1
-    return table.reshape(8 * rows, CH * 16)
+    return table.reshape(4 * rows, CH * 8)
 
 
 def fold_table():
@@ -136,12 +136,13 @@
         return pltpu.make_async_copy(stage.at[rows], out_ref.at[rows], sems.at[b])
 
     def step(b, carry):
-        both = coef[:, pl.ds(pl.multiple_of(b * 32, 32), 32)]
-        sides = [both[:, 16 * e : 16 * e + 16].reshape(16 * CH, XY) for e in range(2)]
-        moved = dot(perm_ref[:, :320], jnp.concatenate(sides, 1)).astype(BF)
-        for e in range(2):
-            at = pl.multiple_of(b * 640 + e * 320, 320)
-            stage[pl.ds(at, 320)] = moved[:, e * XY : (e + 1) * XY]
+        for n in range(2):
+            both = coef[:, pl.ds(pl.multiple_of(b * 32 + n * 16, 16), 16)].astype(F32)
+            sides = [both[:, 8 * e : 8 * e + 8].reshape(8 * CH, XY).astype(BF) for e in range(2)]
+            moved = dot(perm_ref[:160, :160], jnp.concatenate(sides, 1)).astype(BF)
+            for e in range(2):
+                at = pl.multiple_of(b * 640 + n * 320 + e * 160, 160)
+                stage[pl.ds(at, 160)] = moved[:, e * XY : (e + 1) * XY]
         sent(b).start()
         return carry
 
@@ -155,14 +156,15 @@
 
 def unpack(msg_ref, perm_ref, rows, flat, coef):
     def step(b, carry):
-        sides = []
-        for e in range(2):
-            at = pl.multiple_of((2 * b + e) * 8 * rows, 8 * rows)
-            sides.append(msg_ref[pl.ds(at, 8 * rows)])
-        moved = dot(perm_ref[:, : 8 * rows], jnp.concatenate(sides, 1)).astype(BF)
-        for e in range(2):
-            part = moved[:, e * XY : (e + 1) * XY].reshape(CH, 16, XY)
-            flat[:, pl.ds(pl.multiple_of(b * 32 + 16 * e, 16), 16)] = part
+        for n in range(2):
+            sides = []
+            for e in range(2):
+                at = pl.multiple_of((4 * b + 2 * n + e) * 4 * rows, 4 * rows)
+                sides.append(msg_ref[pl.ds(at, 4 * rows)])
+            moved = dot(perm_ref[:160, : 4 * rows], jnp.concatenate(sides, 1))
+            halves = [moved[:, e * XY : (e + 1) * XY].reshape(CH, 8, XY) for e in range(2)]
+            part = jnp.concatenate(halves, 1).astype(BF)
+            flat[:, pl.ds(pl.multiple_of(b * 32 + 16 * n, 16), 16)] = part
         return carry
 
     def turn(n, carry):
@@ -258,8 +260,8 @@
     inverse = plane_tables()[1].astype(np.float32)
     blocks = np.concatenate(np.split(inverse.T, 4), 1)
     perms = np.zeros((512, 1024), np.float32)
-    perms[:320, :320] = pack_table(40).T
-    perms[:320, 384:704] = pack_table(40)
+    perms[:160, :160] = pack_table(40).T
+    perms[:160, 384:544] = pack_table(40)
     return np.concatenate([inverse, blocks, perms], 0)
 
 
@@ -276,7 +278,7 @@
     forward = plane_tables()[0].astype(np.float32).T
     folds = fold_table().reshape(48, 48)
     rest = np.zeros((768, 1024), np.float32)
-    rest[:320, :384] = pack_table(48).T
+    rest[:160, :192] = pack_table(48).T
     rest[320:368, :48] = folds
     return np.concatenate([forward, rest], 0)
 

time: 158 us -> 157 us (level)
  no operation moved by 1% of the time
where the time goes in v3:
time: 157 us; the launch traced here: 156 us
  Pallas kernels  69.6 us (44%)
  waiting for transfers between devices  45 us (29%)
  starting transfers between devices  25.3 us (16%)
  local copies, waits for them, and re-layouts  15.1 us (10%)
    all_to_all x4, waiting for transfers between devices, exchange(): lax.all_to_all(messages, AXES, split_axis=0, concat_axis=0, tiled=True)  45 us
    all_to_all x4, starting transfers between devices, exchange(): lax.all_to_all(messages, AXES, split_axis=0, concat_axis=0, tiled=True)  25.3 us
    pallas_call x2, Pallas kernels, bypass_stage(): call(bypass_kernel, shaped(GRID), limit=60, cost=(FLOPS, 2 * 5 * MIB), gr...  16.4 us
    pallas_call x1, Pallas kernels, tail_stage(): call(tail_kernel, (shaped(FLAT_GRID), shaped(FLAT_GRID), shaped(MESSAGES)...  14.2 us
    pallas_call x1, Pallas kernels, sums_stage(): call(sums_kernel, shaped((1280, 8, 128)), limit=60, cost=(FLOPS, 2 * 5 *...  10.1 us
    pallas_call x1, Pallas kernels, last_stage(): call(last_kernel, (shaped(FLAT_GRID), shaped((CH, CH), F32), shaped((1, C...  7.13 us
    pallas_call x1, Pallas kernels, mix_back_stage(): call(mix_back_kernel, (shaped(WIDE), shaped((SLOTS, *MODE), F32)), limit=...  6.63 us
    pallas_call x1, Pallas kernels, mix_stage(): call(mix_kernel, (shaped(TILES), shaped((SLOTS, *MODE), F32)), limit=LIMI...  6.58 us
  transfers between devices with their start and end apart: 4, of which 4 were waited for; matrix products, arithmetic and copies ran while one was open for 10% of the time, Pallas kernels for 19%

profile of v3, /device:TPU:0, one launch (start us, length us, event | category | flops | bytes accessed | tf_op | source)
XLA Modules:
  0.0 156.1 jit_solution(7086530903153605154)
XLA Ops:
  0.6 5.8 %shard_map.146.after_hbm = bf16[5120,128]{1,0:T(8,128)(2,1)} custom-call(bf16[20,128,1024]{2,1,0:T(8,128)(2,1)} %bitcast.25, bf16[1024,256]{1,0:T(8,128)(2,1)} %constant.15.clone.table_hbm, bf16[160,160]{1,0:T(8,128)(2,1)} %constant.16.clone.perm_hbm), custom_call_target="tpu_custom_call" | custom-call | tf_op jit(solution)/shard_map/pallas_call | solution.py:215
  6.5 11.2 %all-to-all-start = ((bf16[128,40,128]{2,1,0:T(8,128)(2,1)}), bf16[128,40,128]{2,1,0:T(8,128)(2,1)S(1)}, u32[]{:S(2)}, u32[]{:S(2)}) async-start(bf16[128,40,128]{2,1,0:T(8,128)(2,1)} %bitcast.30), calls=%async_computation | async-start | bytes 2621440 | tf_op jit(solution)/shard_map/all_to_all | solution.py:676
  17.6 4.1 %reshape.86 = bf16[2,20,20,8,128]{4,3,0,2,1:T(8,128)(2,1)S(1)} reshape(bf16[2,1,20,20,1024]{4,0,3,2,1:T(2,128)(2,1)} %param.12) | data formatting | bytes 3276800 | tf_op jit(solution)/shard_map/reshape | solution.py:802
  21.7 1.4 copy.19.w_hbm
  23.2 16.3 %all-to-all-done = bf16[128,40,128]{2,1,0:T(8,128)(2,1)S(1)} async-done(((bf16[128,40,128]{2,1,0:T(8,128)(2,1)}), bf16[128,40,128]{2,1,0:T(8,128)(2,1)S(1)}, u32[]{:S(2)}, u32[]{:S(2)}) %all-to-all-start) | async-done | bytes 1310752 | tf_op jit(solution)/shard_map/all_to_all | solution.py:676
  39.4 6.6 %shard_map.147 = (bf16[8,16,5,8,128]{4,3,2,1,0:T(8,128)(2,1)}, f32[13,20,2,8,128]{4,3,2,1,0:T(8,128)}) custom-call(bf16[8,16,5,8,128]{4,3,2,1,0:T(8,128)(2,1)S(1)} %bitcast.23, bf16[2,20,20,8,128]{4,3,2,1,0:T(8,128)(2,1)} %copy.19.w_hbm, bf16[8192,256]{1,0:T(8,128)(2,1)} %constant.14.clone.tables_hbm), custom_call_target="tpu_custom_call" | custom-call | tf_op jit(solution)/shard_map/pallas_call | solution.py:706
  46.0 0.0 copy-start
  46.0 0.0 copy-start.1
  46.0 4.7 %all-to-all-start.1 = ((bf16[128,40,128]{2,1,0:T(8,128)(2,1)}), bf16[128,40,128]{2,1,0:T(8,128)(2,1)S(1)}, u32[]{:S(2)}, u32[]{:S(2)}) async-start(bf16[128,40,128]{2,1,0:T(8,128)(2,1)} %bitcast.3), calls=%async_computation.1 | async-start | bytes 2621440 | tf_op jit(solution)/shard_map/all_to_all | solution.py:676
  50.7 0.0 copy-done
  50.7 0.1 copy.20
  50.8 0.0 copy-done.1
  50.8 0.1 broadcast_in_dim.12
  50.9 0.7 broadcast_in_dim_reshape.4.bias_ref
  51.6 0.2 broadcast_multiply_fusion
  51.8 1.2 mul.44.mix_ref
  53.0 8.1 %shard_map.148 = bf16[20,16,8,1024]{3,2,1,0:T(8,128)(2,1)} custom-call(bf16[5120,128]{1,0:T(8,128)(2,1)} %shard_map.146.after_hbm, bf16[20,16,8,1024]{3,2,1,0:T(8,128)(2,1)} %field_hbm.1, bf16[160,160]{1,0:T(8,128)(2,1)} %mul.44.mix_ref, f32[160,1]{1,0:T(8,128)} %broadcast_in_dim_reshape.4.bias_ref), custom_call_target="tpu_custom_call" | custom-call | flops 1342177280 | bytes 10485760 | tf_op jit(solution)/shard_map/pallas_call | solution.py:718
  61.1 11.3 %all-to-all-done.1 = bf16[128,40,128]{2,1,0:T(8,128)(2,1)S(1)} async-done(((bf16[128,40,128]{2,1,0:T(8,128)(2,1)}), bf16[128,40,128]{2,1,0:T(8,128)(2,1)S(1)}, u32[]{:S(2)}, u32[]{:S(2)}) %all-to-all-start.1) | async-done | bytes 1310752 | tf_op jit(solution)/shard_map/all_to_all | solution.py:676
  72.5 14.2 %shard_map.149 = (bf16[20,128,1024]{2,1,0:T(8,128)(2,1)}, bf16[20,128,1024]{2,1,0:T(8,128)(2,1)}, bf16[5120,128]{1,0:T(8,128)(2,1)}) custom-call(bf16[5120,128]{1,0:T(8,128)(2,1)S(1)} %bitcast.24, bf16[20,128,1024]{2,1,0:T(8,128)(2,1)} %bitcast.29, bf16[20,128,1024]{2,1,0:T(8,128)(2,1)} %bitcast.31, bf16[1024,1024]{1,0:T(8,128)(2,1)} %constant.17.clone.tables_hbm), custom_call_target="tpu_custom_call" | custom-call | flops 2684354560 | bytes 41943040 | tf_op jit(solution)/shard_map/pallas_call | solution.py:731
  86.7 4.8 %all-to-all-start.2 = ((bf16[128,40,128]{2,1,0:T(8,128)(2,1)}), bf16[128,40,128]{2,1,0:T(8,128)(2,1)S(1)}, u32[]{:S(2)}, u32[]{:S(2)}) async-start(bf16[128,40,128]{2,1,0:T(8,128)(2,1)} %bitcast.9), calls=%async_computation.2 | async-start | bytes 2621440 | tf_op jit(solution)/shard_map/all_to_all | solution.py:676
  91.5 10.1 %shard_map.150.sums_hbm = bf16[1280,8,128]{2,1,0:T(8,128)(2,1)} custom-call(bf16[20,16,8,1024]{3,2,1,0:T(8,128)(2,1)} %field_hbm.1, bf16[20,16,8,1024]{3,2,1,0:T(8,128)(2,1)} %bitcast.26, bf16[6,8,48]{2,1,0:T(8,128)(2,1)} %constant.18.clone.fold_ref), custom_call_target="tpu_custom_call" | custom-call | flops 1342177280 | bytes 10485760 | tf_op jit(solution)/shard_map/pallas_call | solution.py:747
  101.6 11.5 %all-to-all-done.2 = bf16[128,40,128]{2,1,0:T(8,128)(2,1)S(1)} async-done(((bf16[128,40,128]{2,1,0:T(8,128)(2,1)}), bf16[128,40,128]{2,1,0:T(8,128)(2,1)S(1)}, u32[]{:S(2)}, u32[]{:S(2)}) %all-to-all-start.2) | async-done | bytes 1310752 | tf_op jit(solution)/shard_map/all_to_all | solution.py:676
  113.1 6.6 %shard_map.151 = (bf16[8,16,6,8,128]{4,3,2,1,0:T(8,128)(2,1)}, f32[13,20,2,8,128]{4,3,2,1,0:T(8,128)}) custom-call(bf16[8,16,5,8,128]{4,3,2,1,0:T(8,128)(2,1)S(1)} %bitcast.22, bf16[2,20,20,8,128]{4,3,2,1,0:T(8,128)(2,1)} %copy.19.w_hbm, bf16[8192,256]{1,0:T(8,128)(2,1)} %constant.14.clone.tables_hbm, bf16[1280,8,128]{2,1,0:T(8,128)(2,1)} %shard_map.150.sums_hbm), custom_call_target="tpu_custom_call" | custom-call | tf_op jit(solution)/shard_map/pallas_call | solution.py:760
  119.7 4.7 %all-to-all-start.3 = ((bf16[128,48,128]{2,1,0:T(8,128)(2,1)}), bf16[128,48,128]{2,1,0:T(8,128)(2,1)S(1)}, u32[]{:S(2)}, u32[]{:S(2)}) async-start(bf16[128,48,128]{2,1,0:T(8,128)(2,1)} %bitcast.12), calls=%async_computation.3 | async-start | bytes 3145728 | tf_op jit(solution)/shard_map/all_to_all | solution.py:676
  124.4 1.2 mul.47.mix_ref
  125.6 0.6 broadcast_in_dim.13.bias_ref
  126.2 8.3 %shard_map.152 = bf16[20,16,8,1024]{3,2,1,0:T(8,128)(2,1)} custom-call(bf16[5120,128]{1,0:T(8,128)(2,1)} %get-tuple-element.17.after_hbm, bf16[20,16,8,1024]{3,2,1,0:T(8,128)(2,1)} %bitcast.27, bf16[160,160]{1,0:T(8,128)(2,1)} %mul.47.mix_ref, f32[160,1]{1,0:T(8,128)} %broadcast_in_dim.13.bias_ref), custom_call_target="tpu_custom_call" | custom-call | flops 1342177280 | bytes 10485760 | tf_op jit(solution)/shard_map/pallas_call | solution.py:718
  134.5 2.7 %shard_map.154 = bf16[2,20,20,8,128]{4,3,2,1,0:T(8,128)(2,1)} custom-call(f32[13,20,2,8,128]{4,3,2,1,0:T(8,128)} %get-tuple-element.21.spec_hbm, f32[13,20,2,8,128]{4,3,2,1,0:T(8,128)} %get-tuple-element.22.back_hbm), custom_call_target="tpu_custom_call" | custom-call | flops 3276800 | bytes 2097152 | tf_op jit(solution)/shard_map/pallas_call | solution.py:771
  137.2 2.8 %reshape.101 = bf16[2,1,20,20,1024]{4,3,2,0,1:T(8,128)(2,1)S(1)} reshape(bf16[2,20,20,8,128]{4,3,2,1,0:T(8,128)(2,1)} %shard_map.154) | data formatting | bytes 3276800 | tf_op jit(solution)/shard_map/reshape | solution.py:818
  140.1 2.9 %copy.24 = bf16[2,1,20,20,1024]{4,0,3,2,1:T(2,128)(2,1)} copy(bf16[2,1,20,20,1024]{4,3,2,0,1:T(8,128)(2,1)S(1)} %reshape.101) | data formatting | bytes 3276800 | tf_op jit(solution)/shard_map/reshape | solution.py:818
  142.9 5.9 %all-to-all-done.3 = bf16[128,48,128]{2,1,0:T(8,128)(2,1)S(1)} async-done(((bf16[128,48,128]{2,1,0:T(8,128)(2,1)}), bf16[128,48,128]{2,1,0:T(8,128)(2,1)S(1)}, u32[]{:S(2)}, u32[]{:S(2)}) %all-to-all-start.3) | async-done | bytes 1572896 | tf_op jit(solution)/shard_map/all_to_all | solution.py:676
  148.8 7.1 %shard_map.153 = (bf16[20,128,1024]{2,1,0:T(8,128)(2,1)}, f32[20,20]{1,0:T(8,128)}, f32[1,20]{1,0:T(1,128)}) custom-call(bf16[6144,128]{1,0:T(8,128)(2,1)S(1)} %bitcast.21, bf16[20,128,1024]{2,1,0:T(8,128)(2,1)} %bitcast.28, bf16[1024,1024]{1,0:T(8,128)(2,1)} %constant.19.clone.tables_hbm), custom_call_target="tpu_custom_call" | custom-call | flops 1342177280 | bytes 10485760 | tf_op jit(solution)/shard_map/pallas_call | solution.py:782
  (1 shorter events, 0.0 us)
Async XLA Ops:
  6.5 32.9 %all-to-all-start = ((bf16[128,40,128]{2,1,0:T(8,128)(2,1)}), bf16[128,40,128]{2,1,0:T(8,128)(2,1)S(1)}, u32[]{:S(2)}, u32[]{:S(2)}) async-start(bf16[128,40,128]{2,1,0:T(8,128)(2,1)} %bitcast.30), calls=%async_computation | async-start | bytes 2621440 | tf_op jit(solution)/shard_map/all_to_all | solution.py:676
  46.0 4.7 %copy-start = (bf16[20,20]{1,0:T(8,128)(2,1)S(1)}, bf16[20,20]{1,0:T(8,128)(2,1)}, u32[]{:S(2)}) copy-start(bf16[20,20]{1,0:T(8,128)(2,1)} %param.13) | copy-start | bytes 2404
  46.0 4.8 %copy-start.1 = (f32[20]{0:T(128)S(1)}, f32[20]{0:T(128)}, u32[]{:S(2)}) copy-start(f32[20]{0:T(128)} %param.14) | copy-start | bytes 244
  46.0 26.4 %all-to-all-start.1 = ((bf16[128,40,128]{2,1,0:T(8,128)(2,1)}), bf16[128,40,128]{2,1,0:T(8,128)(2,1)S(1)}, u32[]{:S(2)}, u32[]{:S(2)}) async-start(bf16[128,40,128]{2,1,0:T(8,128)(2,1)} %bitcast.3), calls=%async_computation.1 | async-start | bytes 2621440 | tf_op jit(solution)/shard_map/all_to_all | solution.py:676
  86.7 26.4 %all-to-all-start.2 = ((bf16[128,40,128]{2,1,0:T(8,128)(2,1)}), bf16[128,40,128]{2,1,0:T(8,128)(2,1)S(1)}, u32[]{:S(2)}, u32[]{:S(2)}) async-start(bf16[128,40,128]{2,1,0:T(8,128)(2,1)} %bitcast.9), calls=%async_computation.2 | async-start | bytes 2621440 | tf_op jit(solution)/shard_map/all_to_all | solution.py:676
  119.7 29.1 %all-to-all-start.3 = ((bf16[128,48,128]{2,1,0:T(8,128)(2,1)}), bf16[128,48,128]{2,1,0:T(8,128)(2,1)S(1)}, u32[]{:S(2)}, u32[]{:S(2)}) async-start(bf16[128,48,128]{2,1,0:T(8,128)(2,1)} %bitcast.12), calls=%async_computation.3 | async-start | bytes 3145728 | tf_op jit(solution)/shard_map/all_to_all | solution.py:676
